TPU v7x, 128 devices: a whole 4x4x4 slice. The times are simulated.
128 devices in a mesh: dp: 32 (over x_lo, z, y), proj: 4 (over x_hi, core).
Axes of the slice: x: 4 (x_hi: 2, x_lo: 2; x = x_hi * 2 + x_lo), y: 4, z: 4, core: 2. Of those that a mesh axis runs over, the one named last changes fastest.
Arguments:
- train_hidden: bfloat16 [8192, 8, 11008], P('dp', None, 'proj'), may hold values from -6 to 6
- train_cotangent: bfloat16 [8192, 8, 4096], P('dp', None, 'proj'), may hold values from -6 to 6
- test_hidden: bfloat16 [4096, 8, 11008], P('dp', None, 'proj'), may hold values from -6 to 6
- test_cotangent: bfloat16 [4096, 8, 4096], P('dp', None, 'proj'), may hold values from -6 to 6
- proj_hidden: bfloat16 [11008, 32], P('proj'), may hold values from -0.0546875 to 0.0546875
- proj_cotangent: bfloat16 [4096, 64], P('proj'), may hold values from -0.09375 to 0.09375
- train_lengths: int32 [8192], P('dp'), may hold values from 1 to 8, as said below
- test_lengths: int32 [4096], P('dp'), may hold values from 1 to 8, as said below
Outputs:
- scores: float32 [8192, 4096], P(('dp', 'proj'))
Inputs may be any that keep to these rules, and one draw needn't show every extreme that they name: `train_lengths`: each example's count of valid tokens; the first example of every set has all 8. `test_lengths`: each example's count of valid tokens; the first example of every set has all 8.
All inputs are finite; a program needn't handle non-finite values.
Results may differ from a plain program's by a relative error of at most 0.029.
Values may be sent and summed in bfloat16 or wider, within the bound.
No kernel may reach another device: no remote copies, remote signals or barrier semaphores. Data moves between devices by JAX's collectives and lax.ppermute only.
A program may use at most 256 MiB of HBM per device.

v0:
```python
import math

import jax
import jax.numpy as jnp
from jax import lax
from jax.sharding import PartitionSpec as P

KG = 64
K = 2048


def project_tokens(hidden, cotangent, proj_hidden, proj_cotangent):
    rows = hidden.shape[0] * hidden.shape[1]
    left = jnp.einsum(
        "fk,rf->kr",
        proj_hidden,
        hidden.reshape(rows, hidden.shape[2]),
        preferred_element_type=jnp.float32,
    )
    right = jnp.einsum(
        "fk,rf->kr",
        proj_cotangent,
        cotangent.reshape(rows, cotangent.shape[2]),
        preferred_element_type=jnp.float32,
    )
    return (left, right)


def build_features(left, right, lengths):
    count = lengths.shape[0]
    toks = left.shape[1] // count
    valid = (jnp.arange(toks, dtype=jnp.int32)[None, :] < lengths[:, None]).astype(jnp.float32)
    left3 = left.reshape(left.shape[0], count, toks) * valid[None, :, :]
    right3 = right.reshape(right.shape[0], count, toks)
    outer = jnp.einsum("bes,aes->eba", right3, left3)
    return outer.reshape(count, right.shape[0] * left.shape[0]).astype(jnp.bfloat16)


def assemble(blocks):
    return lax.all_gather(blocks, "proj", axis=1, tiled=True)


def per_device(
    train_hidden,
    train_cotangent,
    test_hidden,
    test_cotangent,
    proj_hidden,
    proj_cotangent,
    train_lengths,
    test_lengths,
):
    n_proj = lax.axis_size("proj")
    n_dp = lax.axis_size("dp")
    quarter = lax.axis_index("proj")
    width = KG // n_proj
    left_tr, right_tr = project_tokens(train_hidden, train_cotangent, proj_hidden, proj_cotangent)
    left_te, right_te = project_tokens(test_hidden, test_cotangent, proj_hidden, proj_cotangent)
    left_tr, right_tr, left_te, right_te = lax.psum((left_tr, right_tr, left_te, right_te), "proj")
    right_tr = lax.dynamic_slice_in_dim(right_tr, quarter * width, width, 0)
    right_te = lax.dynamic_slice_in_dim(right_te, quarter * width, width, 0)
    mine_tr = build_features(left_tr, right_tr, train_lengths)
    mine_te = build_features(left_te, right_te, test_lengths)
    full_tr, full_te = (
        lax.all_gather(mine_tr, "proj", axis=1, tiled=True),
        lax.all_gather(mine_te, "proj", axis=1, tiled=True),
    )
    partial_value = jnp.dot(full_tr.T, mine_tr, preferred_element_type=jnp.float32)
    summed = lax.psum(partial_value, "dp")
    raw = assemble(summed)
    trace_total = jnp.trace(raw)
    count = train_hidden.shape[0] * n_dp
    damping = 0.1 * trace_total / (count * K)
    gram = raw / count + damping * jnp.eye(K, dtype=jnp.float32)
    factor = jnp.linalg.cholesky(gram)
    share = train_hidden.shape[0] // n_proj
    chosen = lax.dynamic_slice_in_dim(full_tr, quarter * share, share, 0).astype(jnp.float32)
    solved = jax.scipy.linalg.cho_solve((factor, True), chosen.T)
    weighted = solved.T.astype(jnp.bfloat16)
    scale = 1.0 / math.sqrt(K)
    all_tests = lax.all_gather(full_te, "dp", axis=0, tiled=True)
    return (
        lax.dot_general(
            weighted, all_tests, (((1,), (1,)), ((), ())), preferred_element_type=jnp.float32
        )
        * scale
    )


def solution(mesh):
    in_specs = (
        P("dp", None, "proj"),
        P("dp", None, "proj"),
        P("dp", None, "proj"),
        P("dp", None, "proj"),
        P("proj", None),
        P("proj", None),
        P("dp"),
        P("dp"),
    )
    out_specs = P(("dp", "proj"), None)
    return jax.shard_map(
        per_device, mesh=mesh, in_specs=in_specs, out_specs=out_specs, check_vma=False
    )
```

profile of v0, /device:TPU:2, one launch (start us, length us, event | category | flops | bytes accessed | tf_op | source)
XLA Modules:
  0.0 1421.6 jit_solution(5770516657770627753)
XLA Ops:
  6.5 16.5 %copy.46 = bf16[256,8,2752]{2,1,0:T(8,128)(2,1)} copy(bf16[256,8,2752]{0,2,1:T(8,128)(2,1)} %param.8) | data formatting | bytes 22544384 | tf_op args[0]
  47.2 33.6 %all-reduce.10 = (bf16[64,2048]{1,0:T(8,128)(2,1)S(1)}, bf16[64,1024]{1,0:T(8,128)(2,1)S(1)}) all-reduce(f32[64,2048]{1,0:T(8,128)S(1)} %fusion.7, f32[64,1024]{1,0:T(8,128)S(1)} %fusion.44), channel_id=1, replica_groups=mesh['dp'=32,'proj'=4] {'proj'}, use_global_device_ids=true, to_apply=%region_0.0 | all-reduce | flops 196608 | bytes 1179648 | tf_op jit(solution)/shard_map/psum | solution.py:59
  81.3 22.9 %all-reduce.9.cloned.1.call-done = (f32[32,256,8]{0,2,1:T(8,128)}, f32[32,128,8]{0,2,1:T(8,128)}) async-done(((f32[32,256,8]{0,2,1:T(8,128)}, f32[32,128,8]{0,2,1:T(8,128)}), (f32[32,256,8]{0,2,1:T(8,128)}, f32[32,128,8]{0,2,1:T(8,128)})) %all-reduce.9.cloned.1.call-update) | async-done | bytes 393232 | tf_op jit(solution)/shard_map/psum | solution.py:59
  107.9 20.3 %all-gather.4.cloned.1.call-done = bf16[256,2048]{0,1:T(8,128)(2,1)} async-done(((bf16[256,512]{0,1:T(8,128)(2,1)}), bf16[256,2048]{0,1:T(8,128)(2,1)}) %all-gather.4.cloned.1.call-update) | async-done | bytes 1048592 | tf_op jit(solution)/shard_map/all_gather | solution.py:65
  132.3 321.5 %all-reduce.7.cloned.1.call-done = f32[2048,512]{0,1:T(8,128)} async-done(((f32[2048,512]{0,1:T(8,128)}), f32[2048,512]{0,1:T(8,128)}) %all-reduce.7.cloned.1.call-update) | async-done | bytes 4194320 | tf_op jit(solution)/shard_map/psum | solution.py:69
  465.3 100.5 %all-gather.6.cloned.1.call-done = f32[2048,2048]{0,1:T(8,128)} async-done(((f32[2048,512]{0,1:T(8,128)}), f32[2048,2048]{0,1:T(8,128)}) %all-gather.6.cloned.1.call-update) | async-done | bytes 16777232 | tf_op jit(solution)/shard_map/all_gather | solution.py:40
  573.1 12.5 select_add_fusion
  585.6 17.6 %copy.50 = f32[2048,2048]{1,0:T(8,128)} copy(f32[2048,2048]{0,1:T(8,128)} %select_add_fusion) | data formatting | bytes 33554432 | tf_op jit(solution)/shard_map/add | solution.py:74
  603.2 12.2 fusion
  621.2 11.7 cholesky.456
  647.0 11.7 cholesky.479
  683.6 11.7 cholesky.502
  714.3 11.7 cholesky.523
  746.0 11.7 cholesky.960
  844.5 11.9 cholesky.1020
  877.6 11.9 cholesky.1040
  910.6 12.1 cholesky.1060
  943.2 11.9 cholesky.1080
  975.0 11.9 cholesky.1100
  1005.9 12.1 cholesky.1120
  1035.8 11.8 cholesky.1140
  1123.3 12.5 select_select_fusion
  1135.8 58.7 %while.1 = (s32[]{:T(128)}, f32[2048,2048]{0,1:T(8,128)}, s32[16,2]{0,1:T(2,128)S(1)}, f32[16,128,128]{2,1,0:T(8,128)}, s32[]{:T(128)}) while((s32[]{:T(128)}, f32[2048,2048]{0,1:T(8,128)}, s32[16,2]{0,1:T(2,128)S(1)}, f32[16,128,128]{2,1,0:T(8,128)}, s32[]{:T(128)}) %tuple.160), condition=%wide.while_cond, body=%wide.while_body.sunk | while | flops 2 | bytes 393829 | solution.py:78
  1194.5 158.4 %custom-call.145 = f32[16,128,128]{1,2,0:T(8,128)S(1)} custom-call(f32[16,128,128]{2,1,0:T(8,128)} %get-tuple-element.12), custom_call_target="InvertDiagBlocksLowerTriangular" | custom-call | tf_op jit(solution)/shard_map/jit(_cho_solve)/triangular_solve | solution.py:78
  (445 shorter events, 524.8 us)
Async XLA Ops:
  6.5 39.9 %copy-start = (bf16[128,8,1024]{2,1,0:T(8,128)(2,1)S(1)}, bf16[128,8,1024]{2,1,0:T(8,128)(2,1)}, u32[]{:S(2)}) copy-start(bf16[128,8,1024]{2,1,0:T(8,128)(2,1)} %param.11) | copy-start | bytes 6291460
  6.5 25.2 %copy-start.8 = (bf16[2752,32]{0,1:T(8,128)(2,1)S(1)}, bf16[2752,32]{0,1:T(8,128)(2,1)}, u32[]{:S(2)}) copy-start(bf16[2752,32]{0,1:T(8,128)(2,1)} %param.12) | copy-start | bytes 528388
  6.5 97.6 %all-reduce.9.cloned.1.call-start = ((), (), s32[]{:S(2)}) async-start(), calls=%async_computation.4 | async-start | bytes 3145728 | tf_op jit(solution)/shard_map/psum | solution.py:59
  23.1 19.8 %copy-start.9 = (bf16[1024,64]{0,1:T(8,128)(2,1)S(1)}, bf16[1024,64]{0,1:T(8,128)(2,1)}, u32[]{:S(2)}) copy-start(bf16[1024,64]{0,1:T(8,128)(2,1)} %param.13) | copy-start | bytes 393220
  31.7 8.6 copy-start.5
  31.7 49.4 %copy-start.11 = (s32[256]{0:T(256)S(1)}, s32[256]{0:T(256)}, u32[]{:S(2)}) copy-start(s32[256]{0:T(256)} %param.14) | copy-start | bytes 3076
  42.8 411.4 %copy-start.12 = (s32[128]{0:T(128)S(1)}, s32[128]{0:T(128)}, u32[]{:S(2)}) copy-start(s32[128]{0:T(128)} %param.15) | copy-start | bytes 1540
  42.8 85.5 %all-gather.4.cloned.1.call-start = ((), (), s32[]{:S(2)}) async-start(), calls=%async_computation | async-start | bytes 1310720 | tf_op jit(solution)/shard_map/all_gather | solution.py:65
  104.2 350.1 %copy-start.10 = (f32[32,128,8]{0,2,1:T(8,128)S(1)}, f32[32,128,8]{0,2,1:T(8,128)}, u32[]{:S(2)}) copy-start(f32[32,128,8]{0,2,1:T(8,128)} %get-tuple-element.32) | copy-start | bytes 393220
  107.9 346.0 %all-reduce.7.cloned.1.call-start = ((), (), s32[]{:S(2)}) async-start(), calls=%async_computation.1 | async-start | bytes 8388608 | tf_op jit(solution)/shard_map/psum | solution.py:69
  128.2 336.0 %copy-start.6 = (bf16[256,2048]{0,1:T(8,128)(2,1)S(1)}, bf16[256,2048]{0,1:T(8,128)(2,1)}, u32[]{:S(2)}) copy-start(bf16[256,2048]{0,1:T(8,128)(2,1)} %all-gather.4.cloned.1.call-done) | copy-start | bytes 3145732
  132.3 433.4 %all-gather.6.cloned.1.call-start = ((), (), s32[]{:S(2)}) async-start(), calls=%async_computation.2 | async-start | bytes 20971520 | tf_op jit(solution)/shard_map/all_gather | solution.py:40
  453.9 951.1 %all-gather.8.cloned.1.call-start = ((), (), s32[]{:S(2)}) async-start(), calls=%async_computation.3 | async-start | bytes 17301504 | tf_op jit(solution)/shard_map/all_gather | solution.py:81
  615.5 5.7 copy-start.4
  660.2 12.2 copy-start.7
  673.5 5.7 copy-start.2
  1352.9 33.9 %copy-start.3 = (f32[2048,2048]{0,1:T(8,128)S(1)}, f32[2048,2048]{0,1:T(8,128)}, u32[]{:S(2)}) copy-start(f32[2048,2048]{0,1:T(8,128)} %get-tuple-element.271) | copy-start | bytes 50331652
  1398.8 16.0 %copy-start.1 = (bf16[128,8,1024]{2,1,0:T(8,128)(2,1)S(1)}, bf16[128,8,1024]{2,1,0:T(8,128)(2,1)}, u32[]{:S(2)}) copy-start(bf16[128,8,1024]{2,1,0:T(8,128)(2,1)} %param.11) | copy-start | bytes 6291460
Sparse Core Ops, SparseCore 0:
  42.9 61.2 all-reduce.8
  108.0 20.2 all-gather.3
  132.4 321.3 all-reduce.6
  455.4 110.2 all-gather.5
  567.1 244.8 all-gather.7
where the time goes:
time: 1430 us; the launch traced here: 1420 us
  other arithmetic  552 us (39%)
  waiting for transfers between devices  465 us (33%)
  matrix products  206 us (14%)
  local copies, waits for them, and re-layouts  130 us (9%)
  blocking collectives  42.6 us (3%)
  between operations  25.9 us (2%)
    another operation x62, other arithmetic, per_device(): factor = jnp.linalg.cholesky(gram)  348 us
    psum x1, waiting for transfers between devices, per_device(): summed = lax.psum(partial_value, 'dp')  322 us
    another operation x4, other arithmetic, per_device(): solved = jax.scipy.linalg.cho_solve((factor, True), chosen.T)  171 us
    another operation x30, matrix products, per_device(): factor = jnp.linalg.cholesky(gram)  124 us
    all_gather x1, waiting for transfers between devices, assemble(): return lax.all_gather(blocks, 'proj', axis=1, tiled=True)  100 us
    another operation x80, local copies, waits for them, and re-layouts  58.5 us
    another operation x62, matrix products, per_device(): solved = jax.scipy.linalg.cho_solve((factor, True), chosen.T)  49.9 us
    unnamed x117, local copies, waits for them, and re-layouts  37.3 us
  transfers between devices with their start and end apart: 5, of which 4 were waited for; matrix products, arithmetic and copies ran while one was open for 58% of the time, Pallas kernels for 0%

commit v1 on v0

v1 whole, which is shorter than its diff:
```python
import functools
import math

import jax
import jax.numpy as jnp
import numpy as np
from jax import lax
from jax.experimental import pallas as pl
from jax.experimental.pallas import tpu as pltpu
from jax.sharding import PartitionSpec as P

KX = 32
KG = 64
K = 2048
TOKS = 8
COUNT = 8192
GROUP = 256
GROUPS = K // GROUP
EXTRA = 136
TOL = 2.0**-9
START_STEPS = 13
START_FLOPS = 10**9
FINISH_FLOPS = 10**9
MAX_STEPS = 8192

TASKS = [(i, j) for i in range(GROUPS) for j in range(i + 1, GROUPS)]
N_OFF = len(TASKS)
TASKS = TASKS + [(2 * k, 2 * k + 1) for k in range(GROUPS // 2)]

F32 = jnp.float32
BF16 = jnp.bfloat16
CORE_SWAP = [(0, 1), (1, 0), (2, 3), (3, 2)]
FAR_SWAP = [(0, 2), (2, 0), (1, 3), (3, 1)]
NEAR = [[i, i + 16] for i in range(16)]
PLANES = [[h * 16 + i for i in range(16)] for h in range(2)]
SAME_CORE = [[d * 4 + h * 2 + c for d in range(32) for h in range(2)] for c in range(2)]


def vmem_spec():
    return pl.BlockSpec(memory_space=pltpu.VMEM)


def params(mib):
    return pltpu.CompilerParams(vmem_limit_bytes=mib * 1024 * 1024)


def project_kernel(
    at_ref,
    h_ref,
    ht_ref,
    c_ref,
    ct_ref,
    ph_ref,
    pc_ref,
    send_ref,
    keep_ref,
    h,
    ht,
    c,
    ct,
    ph,
    pc,
    left,
    left_te,
    right,
    right_te,
    chunks,
    sems,
):
    def token(t):
        return (
            pltpu.make_async_copy(h_ref.at[t], h.at[t], sems.at[4 + t]),
            pltpu.make_async_copy(ht_ref.at[t], ht.at[t], sems.at[4 + TOKS + t]),
        )

    first = [
        pltpu.make_async_copy(src, dst, sems.at[n])
        for n, (src, dst) in enumerate([(pc_ref, pc), (c_ref, c), (ct_ref, ct), (ph_ref, ph)])
    ]
    for copy in first:
        copy.start()
    for t in range(TOKS):
        for copy in token(t):
            copy.start()

    nt = (((1,), (1,)), ((), ()))
    first[0].wait()
    for n, src, dst, slots, base in ((1, c, right, 4, 0), (2, ct, right_te, 2, 4)):
        first[n].wait()
        dst[:, 0:KG] = lax.dot_general(src[...], pc[...], nt, preferred_element_type=F32)
        examples = dst.shape[0] // TOKS
        parts = TOKS // slots
        width = examples // 4
        for u in range(slots):
            tall = [dst[pl.ds(p * slots + u, examples, stride=TOKS), :].T for p in range(parts)]
            for q in range(4):
                chunks[q, base + u, KX : KX + KG, :] = jnp.concatenate(
                    [piece[0:KG, width * q : width * (q + 1)] for piece in tall], axis=1
                )
    first[3].wait()

    def step(t, carry):
        for copy in token(t):
            copy.wait()
        left[t] = jnp.dot(ph[...], h[t], preferred_element_type=F32)
        left_te[t] = jnp.dot(ph[...], ht[t], preferred_element_type=F32)
        return carry

    lax.fori_loop(0, TOKS, step, 0)
    for src, slots, base in ((left, 4, 0), (left_te, 2, 4)):
        parts = TOKS // slots
        width = src.shape[2] // 4
        for u in range(slots):
            for q in range(4):
                chunks[q, base + u, 0:KX, :] = jnp.concatenate(
                    [src[p * slots + u, :, width * q : width * (q + 1)] for p in range(parts)],
                    axis=1,
                )
    for q in range(4):
        side, core = divmod(q, 2)
        slot = jnp.where(at_ref[1] == side, 0, 1)

        @pl.when(at_ref[0] == core)
        def _():
            keep_ref[slot] = chunks[q]

        @pl.when(at_ref[0] != core)
        def _():
            send_ref[slot] = chunks[q]


def project(at, hidden, hidden_te, cot, cot_te, ph, pc):
    shape = jax.ShapeDtypeStruct((2, 6, KX + KG, 128), F32)
    arrays = [hidden, hidden_te, cot, cot_te, ph, pc]
    any_spec = pl.BlockSpec(memory_space=pl.ANY)
    return pl.pallas_call(
        project_kernel,
        in_specs=[pl.BlockSpec(memory_space=pltpu.SMEM)] + [any_spec] * 6,
        out_specs=[vmem_spec()] * 2,
        out_shape=[shape, shape],
        scratch_shapes=[pltpu.VMEM(array.shape, BF16) for array in arrays]
        + [
            pltpu.VMEM((TOKS, KX, 256), F32),
            pltpu.VMEM((TOKS, KX, 128), F32),
            pltpu.VMEM((2048, 128), F32),
            pltpu.VMEM((1024, 128), F32),
            pltpu.VMEM((4, 6, KX + KG, 128), F32),
            pltpu.SemaphoreType.DMA((4 + 2 * TOKS,)),
        ],
        compiler_params=params(60),
        cost_estimate=pl.CostEstimate(flops=10**9, bytes_accessed=3 * 10**7, transcendentals=0),
        name="project",
    )(at, *arrays)


def feature_kernel(mine_ref, got_ref, lens_ref, train_ref, test_ref, send_ref, right, feat):
    for base, slots, out_ref in ((0, 4, train_ref), (4, 2, test_ref)):
        parts = TOKS // slots
        width = 128 // parts
        lens = lens_ref[base // 4 : base // 4 + 1, :]
        part = lax.broadcasted_iota(jnp.int32, (1, 128), 1) // width
        left = []
        for u in range(slots):
            at = base + u
            valid = lens > part * slots + u
            left.append(jnp.where(valid, mine_ref[at, 0:KX, :] + got_ref[at, 0:KX, :], 0.0))
            right[u] = mine_ref[at, KX : KX + KG, :] + got_ref[at, KX : KX + KG, :]
        for j in range(KG):
            acc = left[0] * right[0, j : j + 1, :]
            for u in range(1, slots):
                acc += left[u] * right[u, j : j + 1, :]
            feat[j * KX : (j + 1) * KX, :] = acc
        for k in range(K // 128):
            tall = feat[k * 128 : (k + 1) * 128, :].T
            block = tall[0:width]
            for p in range(1, parts):
                block += tall[p * width : (p + 1) * width]
            block = block.astype(BF16)
            out_ref[:, k * 128 : (k + 1) * 128] = block
            if base:
                continue
            group, off = divmod(k * 128, GROUP)
            for n, (i, j) in enumerate(TASKS):
                if i == group:
                    send_ref[n, :, off : off + 128] = block
                if j == group:
                    send_ref[n, :, GROUP + off : GROUP + off + 128] = block


def features(mine, got, lens):
    return pl.pallas_call(
        feature_kernel,
        in_specs=[vmem_spec()] * 3,
        out_specs=[vmem_spec()] * 3,
        out_shape=[
            jax.ShapeDtypeStruct((64, K), BF16),
            jax.ShapeDtypeStruct((32, K), BF16),
            jax.ShapeDtypeStruct((32, 64, 2 * GROUP), BF16),
        ],
        scratch_shapes=[pltpu.VMEM((4, KG, 128), F32), pltpu.VMEM((K, 128), F32)],
        compiler_params=params(40),
        name="features",
    )(mine, got, lens)


def gram_kernel(at_ref, rows_ref, send_ref, keep_ref, block, tail):
    left = rows_ref[:, 0:GROUP]
    right = rows_ref[:, GROUP : 2 * GROUP]
    tn = (((0,), (0,)), ((), ()))
    tail[...] = jnp.zeros((EXTRA - 128, 128), F32)

    @pl.when(at_ref[2] == 0)
    def _():
        block[...] = lax.dot_general(left, right, tn, preferred_element_type=F32)

    @pl.when(at_ref[2] == 1)
    def _():
        low = lax.dot_general(left, left, tn, preferred_element_type=F32)
        high = lax.dot_general(right, right, tn, preferred_element_type=F32)
        row = lax.broadcasted_iota(jnp.int32, (GROUP, GROUP), 0)
        col = lax.broadcasted_iota(jnp.int32, (GROUP, GROUP), 1)
        block[...] = jnp.where(row >= col, low, high)
        diag = jnp.sum(jnp.where(row == col, high, 0.0), axis=0, keepdims=True)
        tail[0:1, :] = diag[:, 0:128]
        tail[1:2, :] = diag[:, 128:256]

    def fill(ref, slot, q):
        ref[slot, 0:64, :] = block[64 * q : 64 * q + 64, 0:128]
        ref[slot, 64:128, :] = block[64 * q : 64 * q + 64, 128:256]
        ref[slot, 128:EXTRA, :] = tail[...]

    for q in range(4):
        side, core = divmod(q, 2)
        slot = jnp.where(at_ref[1] == side, 0, 1)

        @pl.when(at_ref[0] == core)
        def _():
            fill(keep_ref, slot, q)

        @pl.when(at_ref[0] != core)
        def _():
            fill(send_ref, slot, q)


def gram_block(at, rows):
    shape = jax.ShapeDtypeStruct((2, EXTRA, 128), F32)
    return pl.pallas_call(
        gram_kernel,
        in_specs=[pl.BlockSpec(memory_space=pltpu.SMEM), vmem_spec()],
        out_specs=[vmem_spec()] * 2,
        out_shape=[shape, shape],
        scratch_shapes=[pltpu.VMEM((GROUP, GROUP), F32), pltpu.VMEM((EXTRA - 128, 128), F32)],
        compiler_params=params(40),
        name="gram_block",
    )(at, rows)


def split_kernel(want_low, mine_ref, got_ref, out_ref):
    total = mine_ref[...] + got_ref[...]
    part = total.astype(BF16)
    if want_low:
        part = (total - part.astype(F32)).astype(BF16)
    for n in range(64):
        out_ref[n] = part


def split(mine, got, want_low):
    return pl.pallas_call(
        functools.partial(split_kernel, want_low),
        in_specs=[vmem_spec()] * 2,
        out_specs=vmem_spec(),
        out_shape=jax.ShapeDtypeStruct((64, EXTRA, 128), BF16),
        compiler_params=params(60),
        name="split_low" if want_low else "split_high",
    )(mine, got)


def unpack(core, own, other, out, trace_ref):
    @pl.when(core == 0)
    def _():
        unpack_parts((own, other), out, trace_ref)

    @pl.when(core == 1)
    def _():
        unpack_parts((other, own), out, trace_ref)

    return jnp.sum(trace_ref[0:1, :], axis=1, keepdims=True)


def unpack_parts(parts, out, trace_ref):
    row = lax.broadcasted_iota(jnp.int32, (GROUP, GROUP), 0)
    col = lax.broadcasted_iota(jnp.int32, (GROUP, GROUP), 1)
    trace = jnp.zeros((1, GROUP), F32)
    for n, (i, j) in enumerate(TASKS):
        pieces = []
        for q in range(4):
            h, c = divmod(q, 2)
            pieces.append(
                jnp.concatenate(
                    [parts[c][2 * n + h, 0:64, :], parts[c][2 * n + h, 64:128, :]], axis=1
                )
            )
        block = jnp.concatenate(pieces, axis=0)
        i0, j0 = i * GROUP, j * GROUP
        if n < N_OFF:
            out[i0 : i0 + GROUP, j0 : j0 + GROUP] = block
            out[j0 : j0 + GROUP, i0 : i0 + GROUP] = block.T
        else:
            wide = block.astype(F32)
            flipped = wide.T
            tail = parts[0][2 * n, 128:EXTRA, :].astype(F32)
            diag = jnp.concatenate([tail[0:1], tail[1:2]], axis=1)
            low = jnp.where(row >= col, wide, flipped)
            high = jnp.where(row < col, wide, jnp.where(row > col, flipped, diag))
            trace += jnp.sum(jnp.where(row == col, wide, 0.0), axis=0, keepdims=True) + diag
            out[i0 : i0 + GROUP, i0 : i0 + GROUP] = low.astype(BF16)
            out[j0 : j0 + GROUP, j0 : j0 + GROUP] = high.astype(BF16)
    trace_ref[0:1, :] = trace


def rows_dot(a, b):
    return jnp.sum(a * b, axis=1, keepdims=True)


BLOCKS = [slice(n * GROUP, (n + 1) * GROUP) for n in range(GROUPS)]


def product(high, low, p, y, gain):
    upper = [p[:, cols].astype(BF16) for cols in BLOCKS]
    left = jnp.concatenate(upper, axis=1)
    if low is not None:
        lower = [(p[:, cols] - up.astype(F32)).astype(BF16) for cols, up in zip(BLOCKS, upper)]
        both = jnp.concatenate([left, jnp.concatenate(lower, axis=1)], axis=0)
    total = jnp.zeros((64, GROUP), F32)
    for cols in BLOCKS:
        if low is None:
            main = jnp.dot(left, high[:, cols], preferred_element_type=F32)
        else:
            main = jnp.dot(both, high[:, cols], preferred_element_type=F32)
            rest = jnp.dot(left, low[:, cols], preferred_element_type=F32)
            main = main[0:64] + main[64:128] + rest
        value = main * gain + 0.1 * p[:, cols]
        y[:, cols] = value
        total += value * p[:, cols]
    return jnp.sum(total, axis=1, keepdims=True)


def advance(high, low, x, r, p, y, gain, rr):
    py = product(high, low, p, y, gain)
    alpha = jnp.where(py > 0.0, rr / jnp.where(py > 0.0, py, 1.0), 0.0)
    new = jnp.zeros((64, GROUP), F32)
    xx = jnp.zeros((64, GROUP), F32)
    for cols in BLOCKS:
        xv = x[:, cols] + alpha * p[:, cols]
        rv = r[:, cols] - alpha * y[:, cols]
        x[:, cols] = xv
        r[:, cols] = rv
        xx += xv * xv
        new += rv * rv
    new = jnp.sum(new, axis=1, keepdims=True)
    beta = new / jnp.where(rr > 0.0, rr, 1.0)
    for cols in BLOCKS:
        p[:, cols] = r[:, cols] + beta * p[:, cols]
    return new, jnp.sum(xx, axis=1, keepdims=True)


def scaled(f_ref):
    f = f_ref[...].astype(F32)
    top = jnp.max(jnp.abs(f), axis=1, keepdims=True)
    top = jnp.where(top > 0.0, top, 1.0)
    return f / top, top


def start_kernel(
    core_ref, own, other, f_ref, x0_ref, base_ref, trace_ref, gram, high, x, r, p, y, sem
):
    f, _ = scaled(f_ref)
    r[...] = f
    p[...] = f
    x[...] = jnp.zeros_like(f)
    gain = K / unpack(core_ref[0], own, other, high, trace_ref)
    keep = pltpu.make_async_copy(high, gram, sem)
    keep.start()
    lax.fori_loop(
        0,
        START_STEPS,
        lambda _, rr: advance(high, None, x, r, p, y, gain, rr)[0],
        rows_dot(f, f),
    )
    x0 = x[...].astype(BF16)
    x0_ref[...] = x0
    for cols in BLOCKS:
        base_ref[:, cols] = jnp.dot(x0, high[:, cols], preferred_element_type=F32)
    keep.wait()


def solve_start(core, own, other, f):
    return pl.pallas_call(
        start_kernel,
        in_specs=[pl.BlockSpec(memory_space=pltpu.SMEM)] + [vmem_spec()] * 3,
        out_specs=[vmem_spec()] * 3 + [pl.BlockSpec(memory_space=pl.ANY)],
        out_shape=[
            jax.ShapeDtypeStruct((64, K), BF16),
            jax.ShapeDtypeStruct((64, K), F32),
            jax.ShapeDtypeStruct((8, GROUP), F32),
            jax.ShapeDtypeStruct((K, K), BF16),
        ],
        scratch_shapes=[
            pltpu.VMEM((K, K), BF16),
            pltpu.VMEM((64, K), F32),
            pltpu.VMEM((64, K), F32),
            pltpu.VMEM((64, K), F32),
            pltpu.VMEM((64, K), F32),
            pltpu.SemaphoreType.DMA,
        ],
        cost_estimate=pl.CostEstimate(flops=START_FLOPS, bytes_accessed=10**7, transcendentals=0),
        compiler_params=params(60),
        name="solve_start",
    )(core, own, other, f)


def finish_kernel(
    core_ref,
    own,
    other,
    gram,
    f_ref,
    x0_ref,
    base_ref,
    trace_ref,
    w_ref,
    high,
    low,
    low_trace,
    x,
    r,
    p,
    y,
    sem,
):
    load = pltpu.make_async_copy(gram, high, sem)
    load.start()
    f, top = scaled(f_ref)
    trace = jnp.sum(trace_ref[0:1, :], axis=1, keepdims=True)
    trace = trace + unpack(core_ref[0], own, other, low, low_trace)
    gain = K / trace
    x0 = x0_ref[...]
    for cols in BLOCKS:
        main = base_ref[:, cols] + jnp.dot(x0, low[:, cols], preferred_element_type=F32)
        y[:, cols] = main * gain + 0.1 * x0_ref[:, cols].astype(F32)
    ff = rows_dot(f, f)
    rest = f - y[...]
    rr = rows_dot(rest, rest)
    good = rr <= ff
    rr = jnp.where(good, rr, ff)
    first = jnp.where(good, x0.astype(F32), 0.0)
    rest = jnp.where(good, rest, f)
    x[...] = first
    r[...] = rest
    p[...] = rest
    load.wait()

    def excess(rr, xx):
        return jnp.max(rr - (0.1 * TOL) ** 2 * xx)

    def more(state):
        return jnp.logical_and(state[0] < MAX_STEPS, state[2] > 0.0)

    def body(state):
        step, rr, _ = state
        rr, xx = advance(high, low, x, r, p, y, gain, rr)
        return step + 1, rr, excess(rr, xx)

    lax.while_loop(more, body, (jnp.int32(0), rr, excess(rr, rows_dot(first, first))))
    w_ref[...] = (x[...] * (top * (COUNT * K / trace))).astype(BF16)


def solve_finish(core, own, other, high, f, x0, base, trace):
    return pl.pallas_call(
        finish_kernel,
        in_specs=[pl.BlockSpec(memory_space=pltpu.SMEM)] + [vmem_spec()] * 2
        + [pl.BlockSpec(memory_space=pl.ANY)]
        + [vmem_spec()] * 4,
        out_specs=vmem_spec(),
        out_shape=jax.ShapeDtypeStruct((64, K), BF16),
        scratch_shapes=[
            pltpu.VMEM((K, K), BF16),
            pltpu.VMEM((K, K), BF16),
            pltpu.VMEM((8, GROUP), F32),
            pltpu.VMEM((64, K), F32),
            pltpu.VMEM((64, K), F32),
            pltpu.VMEM((64, K), F32),
            pltpu.VMEM((64, K), F32),
            pltpu.SemaphoreType.DMA,
        ],
        cost_estimate=pl.CostEstimate(flops=FINISH_FLOPS, bytes_accessed=10**7, transcendentals=0),
        compiler_params=params(46),
        name="solve_finish",
    )(core, own, other, high, f, x0, base, trace)


def place_kernel(place_ref, *refs):
    out_ref = refs[-1]
    for me in range(4):

        @pl.when(2 * place_ref[1] + place_ref[0] == me)
        def _():
            for d in range(32):
                at = 64 * (d % 16) + 32 * (d // 16)
                out_ref[:, 128 * d : 128 * d + 128] = jnp.concatenate(
                    [refs[me ^ q][:, at : at + 32].astype(F32) for q in range(4)], axis=1
                )


def place(index, parts):
    return pl.pallas_call(
        place_kernel,
        in_specs=[pl.BlockSpec(memory_space=pltpu.SMEM)] + [vmem_spec()] * 4,
        out_specs=vmem_spec(),
        out_shape=jax.ShapeDtypeStruct((64, 4096), F32),
        compiler_params=params(40),
        name="place",
    )(index, *parts)


def fold(send, keep):
    recv = lax.ppermute(send, "proj", CORE_SWAP)
    return keep[0] + recv[0], lax.ppermute(keep[1] + recv[1], "proj", FAR_SWAP)


def exchange(chunks):
    return lax.all_to_all(
        chunks, ("dp", "proj"), 0, 0, axis_index_groups=SAME_CORE, tiled=True
    )


def per_device(
    train_hidden,
    train_cotangent,
    test_hidden,
    test_cotangent,
    proj_hidden,
    proj_cotangent,
    train_lengths,
    test_lengths,
):
    quarter = lax.axis_index("proj").astype(jnp.uint32)
    far, core = (quarter >> 1).astype(jnp.int32), (quarter & 1).astype(jnp.int32)
    task = lax.axis_index("dp")
    d = train_cotangent.shape[2]
    at = jnp.stack([core, far, (task >= N_OFF).astype(jnp.int32), core * 0])
    ph, pc = proj_hidden.T, proj_cotangent.T
    send, keep = project(
        at,
        jnp.transpose(train_hidden, (1, 2, 0)),
        jnp.transpose(test_hidden, (1, 2, 0)),
        train_cotangent.reshape(-1, d),
        test_cotangent.reshape(-1, d),
        ph,
        pc,
    )
    lens = jnp.stack(
        [
            jnp.tile(lax.dynamic_slice_in_dim(train_lengths, quarter * 64, 64), 2),
            jnp.tile(lax.dynamic_slice_in_dim(test_lengths, quarter * 32, 32), 4),
        ]
    )
    train, test, send = features(*fold(send, keep), lens)
    pairs = lax.all_gather(test, "dp", axis_index_groups=NEAR, axis=0, tiled=True)
    rows = lax.all_to_all(send, "dp", 0, 0, tiled=True).reshape(2048, 2 * GROUP)
    rows, pairs = lax.optimization_barrier((rows, pairs))
    tests = lax.all_gather(pairs, "dp", axis_index_groups=PLANES, axis=0, tiled=True)
    mine, got = fold(*gram_block(at, rows))
    high, low = split(mine, got, False), split(mine, got, True)
    high_own, low = lax.optimization_barrier((exchange(high), low))
    high_other = lax.ppermute(high_own, "proj", CORE_SWAP)
    low_own = exchange(low)
    x0, base, trace, gram = solve_start(at, high_own, high_other, train)
    low_own, x0 = lax.optimization_barrier((low_own, x0))
    low_other = lax.ppermute(low_own, "proj", CORE_SWAP)
    weighted = solve_finish(at, low_own, low_other, gram, train, x0, base, trace)
    weighted, tests = lax.optimization_barrier((weighted, tests))
    beyond = lax.ppermute(weighted, "proj", FAR_SWAP)
    tests_other = lax.ppermute(tests, "proj", CORE_SWAP)
    scale = 1.0 / math.sqrt(K)

    def scores(w, t):
        nt = (((1,), (1,)), ((), ()))
        return lax.dot_general(w, t, nt, preferred_element_type=F32) * scale

    near = scores(weighted, tests)
    beyond, near = lax.optimization_barrier((beyond, near))
    sent = jnp.concatenate([scores(beyond, tests), scores(beyond, tests_other)], axis=1)
    got = lax.ppermute(sent.astype(BF16), "proj", FAR_SWAP)
    return place(
        at,
        [near, scores(weighted, tests_other), got[:, 0:1024], got[:, 1024:]],
    )


def solution(mesh):
    in_specs = (
        P("dp", None, "proj"),
        P("dp", None, "proj"),
        P("dp", None, "proj"),
        P("dp", None, "proj"),
        P("proj", None),
        P("proj", None),
        P("dp"),
        P("dp"),
    )
    out_specs = P(("dp", "proj"), None)
    return jax.shard_map(
        per_device, mesh=mesh, in_specs=in_specs, out_specs=out_specs, check_vma=False
    )
```

time: 1430 us -> 304 us (0.21)
  other arithmetic: 552 us -> 2.36 us
  waiting for transfers between devices: 465 us -> 61.9 us
  matrix products: 206 us -> 7.77 us
  Pallas kernels: 0 us -> 149 us
  local copies, waits for them, and re-layouts: 130 us -> 5.71 us
  starting transfers between devices: 0.17 us -> 36.1 us
  blocking collectives: 42.6 us -> 25.5 us
    another operation x66 -> x2, other arithmetic: 519 us -> 0.57 us  [the longest x1 0.56 us: per_device(): at = jnp.stack([core, far, (task >= N_OFF).astype(jnp.int32), core * 0])]
    psum x2 -> x0, waiting for transfers between devices: 344 us -> none  [the longest x1 322 us: per_device(): summed = lax.psum(partial_value, 'dp')]
    another operation x92 -> x0, matrix products: 174 us -> none  [the longest x30 124 us: per_device(): factor = jnp.linalg.cholesky(gram)]
    pallas_call x0 -> x8, Pallas kernels: none -> 149 us  [the longest x1 97.4 us: solve_finish(): pl.pallas_call(finish_kernel, in_specs=[pl.BlockSpec(memory_space=pltpu.S...]
    all_gather x3 -> x1, waiting for transfers between devices: 121 us -> 0.02 us  [per_device(): lax.all_gather(pairs, 'dp', axis_index_groups=PLANES, axis=0, tiled=True)]
    another operation x141 -> x4, local copies, waits for them, and re-layouts: 72.7 us -> 0.18 us  [the longest x2 0.17 us: per_device(): jnp.stack([jnp.tile(lax.dynamic_slice_in_dim(train_lengths, quarter * 64,...]
    all_to_all x0 -> x3, waiting for transfers between devices: none -> 34.5 us  [the longest x2 32.4 us: exchange(): lax.all_to_all(chunks, ('dp', 'proj'), 0, 0, axis_index_groups=SAME_CORE,...]
    psum x1 -> x0, blocking collectives: 33.6 us -> none  [per_device(): lax.psum((left_tr, right_tr, left_te, right_te), 'proj')]
  transfers between devices with their start and end apart: 5 -> 13, of which waited for: 4 -> 10; matrix products, arithmetic and copies ran while one was open for 58% -> 2% of each run, Pallas kernels for 0% -> 44%
where the time goes in v1:
time: 304 us; the launch traced here: 302 us
  Pallas kernels  149 us (49%)
  waiting for transfers between devices  61.9 us (20%)
  starting transfers between devices  36.1 us (12%)
  blocking collectives  25.5 us (8%)
  between operations  13.6 us (4%)
  matrix products  7.77 us (3%)
  local copies, waits for them, and re-layouts  5.71 us (2%)
    pallas_call x1, Pallas kernels, solve_finish(): pl.pallas_call(finish_kernel, in_specs=[pl.BlockSpec(memory_space=pltpu.S...  97.4 us
    all_to_all x2, waiting for transfers between devices, exchange(): lax.all_to_all(chunks, ('dp', 'proj'), 0, 0, axis_index_groups=SAME_CORE,...  32.4 us
    pallas_call x1, Pallas kernels, solve_start(): pl.pallas_call(start_kernel, in_specs=[pl.BlockSpec(memory_space=pltpu.SM...  30.5 us
    all_gather x1, blocking collectives, per_device(): lax.all_gather(test, 'dp', axis_index_groups=NEAR, axis=0, tiled=True)  25.5 us
    all_to_all x2, starting transfers between devices, exchange(): lax.all_to_all(chunks, ('dp', 'proj'), 0, 0, axis_index_groups=SAME_CORE,...  15.2 us
    pallas_call x1, Pallas kernels, project(): pl.pallas_call(project_kernel, in_specs=[pl.BlockSpec(memory_space=pltpu....  11.8 us
    ppermute x2, waiting for transfers between devices, fold(): lax.ppermute(keep[1] + recv[1], 'proj', FAR_SWAP)  11.8 us
    all_to_all x1, starting transfers between devices, per_device(): rows = lax.all_to_all(send, 'dp', 0, 0, tiled=True).reshape(2048, 2 * GROUP)  9.57 us
  transfers between devices with their start and end apart: 13, of which 10 were waited for; matrix products, arithmetic and copies ran while one was open for 2% of the time, Pallas kernels for 44%

profile of v1, /device:TPU:2, one launch (start us, length us, event | category | flops | bytes accessed | tf_op | source)
XLA Modules:
  0.0 301.7 jit_solution(3286467528043664523)
XLA Ops:
  7.1 11.8 %project.1 = (f32[2,6,96,128]{3,2,1,0:T(8,128)}, f32[2,6,96,128]{3,2,1,0:T(8,128)}) custom-call(s32[4]{0:T(128)} %pad_add_fusion.1.at_ref.core_ref.place_ref, bf16[8,2752,256]{2,1,0:T(8,128)(2,1)} %bitcast.27, bf16[8,2752,128]{2,1,0:T(8,128)(2,1)} %bitcast.28, bf16[2048,1024]{1,0:T(8,128)(2,1)} %bitcast.29, bf16[1024,1024]{1,0:T(8,128)(2,1)} %bitcast.30, ...), custom_call_target="tpu_custom_call" | custom-call | flops 1000000000 | bytes 30000000 | tf_op jit(solution)/shard_map/project/pallas_call | solution.py:136
  19.1 2.2 collective-permute-done
  22.4 2.2 collective-permute-start.1
  24.9 8.1 %collective-permute-done.1.got_ref = f32[6,96,128]{2,1,0:T(8,128)S(1)} collective-permute-done((f32[6,96,128]{2,1,0:T(8,128)S(1)}, f32[6,96,128]{2,1,0:T(8,128)S(1)}, u32[]{:S(2)}, u32[]{:S(2)}) %collective-permute-start.1) | collective-permute-done | bytes 294944 | tf_op jit(solution)/shard_map/ppermute | solution.py:528
  35.8 9.6 %all-to-all-start = ((bf16[32,64,512]{2,1,0:T(8,128)(2,1)}), bf16[32,64,512]{2,1,0:T(8,128)(2,1)S(1)}, u32[]{:S(2)}, u32[]{:S(2)}) async-start(bf16[32,64,512]{2,1,0:T(8,128)(2,1)} %copy-done), calls=%async_computation | async-start | bytes 4194304 | tf_op jit(solution)/shard_map/all_to_all | solution.py:570
  45.4 25.5 %all_gather.6 = bf16[64,2048]{1,0:T(8,128)(2,1)} all-gather(bf16[32,2048]{1,0:T(8,128)(2,1)S(1)} %get-tuple-element.29), channel_id=1, replica_groups={{0,64},{4,68},{8,72},{12,76},{16,80},{20,84},{24,88},{28,92},{32,96},{3..., dimensions={0}, use_global_device_ids=true | all-gather | bytes 393216 | tf_op jit(solution)/shard_map/all_gather | solution.py:569
  70.9 2.1 all-to-all-done
  76.3 2.1 collective-permute-start.3
  78.5 3.7 %collective-permute-done.3.got_ref = f32[136,128]{1,0:T(8,128)S(1)} collective-permute-done((f32[136,128]{1,0:T(8,128)S(1)}, f32[136,128]{1,0:T(8,128)S(1)}, u32[]{:S(2)}, u32[]{:S(2)}) %collective-permute-start.3) | collective-permute-done | bytes 69664 | tf_op jit(solution)/shard_map/ppermute | solution.py:528
  82.8 2.5 split_high.1
  85.2 9.3 %all-to-all-start.1 = ((bf16[64,136,128]{2,1,0:T(8,128)(2,1)}), bf16[64,136,128]{2,1,0:T(8,128)(2,1)}, u32[]{:S(2)}, u32[]{:S(2)}) async-start(bf16[64,136,128]{2,1,0:T(8,128)(2,1)} %split_high.1), calls=%async_computation.1 | async-start | bytes 4456448 | tf_op jit(solution)/shard_map/all_to_all | solution.py:532
  94.5 2.4 split_low.1
  96.9 26.6 %all-to-all-done.1.own = bf16[64,136,128]{2,1,0:T(8,128)(2,1)} async-done(((bf16[64,136,128]{2,1,0:T(8,128)(2,1)}), bf16[64,136,128]{2,1,0:T(8,128)(2,1)}, u32[]{:S(2)}, u32[]{:S(2)}) %all-to-all-start.1) | async-done | bytes 2228256 | tf_op jit(solution)/shard_map/all_to_all | solution.py:532
  123.5 6.0 %all-to-all-start.2 = ((bf16[64,136,128]{2,1,0:T(8,128)(2,1)}), bf16[64,136,128]{2,1,0:T(8,128)(2,1)S(1)}, u32[]{:S(2)}, u32[]{:S(2)}) async-start(bf16[64,136,128]{2,1,0:T(8,128)(2,1)} %split_low.1), calls=%async_computation.2 | async-start | bytes 4456448 | tf_op jit(solution)/shard_map/all_to_all | solution.py:532
  129.5 30.5 %solve_start.1 = (bf16[64,2048]{1,0:T(8,128)(2,1)}, f32[64,2048]{1,0:T(8,128)}, f32[8,256]{1,0:T(8,128)}, bf16[2048,2048]{1,0:T(8,128)(2,1)}) custom-call(s32[4]{0:T(128)} %pad_add_fusion.1.at_ref.core_ref.place_ref, bf16[64,136,128]{2,1,0:T(8,128)(2,1)} %all-to-all-done.1.own, bf16[64,136,128]{2,1,0:T(8,128)(2,1)} %collective-permute-done.4.other, ...), custom_call_target="tpu_custom_call" | custom-call | flops 1000000000 | bytes 10000000 | tf_op jit(solution)/shard_map/solve_start/pallas_call | solution.py:398
  160.0 5.8 %all-to-all-done.2.own = bf16[64,136,128]{2,1,0:T(8,128)(2,1)S(1)} async-done(((bf16[64,136,128]{2,1,0:T(8,128)(2,1)}), bf16[64,136,128]{2,1,0:T(8,128)(2,1)S(1)}, u32[]{:S(2)}, u32[]{:S(2)}) %all-to-all-start.2) | async-done | bytes 2228256 | tf_op jit(solution)/shard_map/all_to_all | solution.py:532
  165.8 4.3 %collective-permute-done.5.other = bf16[64,136,128]{2,1,0:T(8,128)(2,1)S(1)} collective-permute-done((bf16[64,136,128]{2,1,0:T(8,128)(2,1)S(1)}, bf16[64,136,128]{2,1,0:T(8,128)(2,1)S(1)}, u32[]{:S(2)}, u32[]{:S(2)}) %collective-permute-start.5) | collective-permute-done | bytes 2228256 | tf_op jit(solution)/shard_map/ppermute | solution.py:580
  172.9 97.4 %solve_finish.1 = bf16[64,2048]{1,0:T(8,128)(2,1)S(1)} custom-call(s32[4]{0:T(128)S(1)} %copy-done.6, bf16[64,136,128]{2,1,0:T(8,128)(2,1)S(1)} %all-to-all-done.2.own, bf16[64,136,128]{2,1,0:T(8,128)(2,1)S(1)} %collective-permute-done.5.other, bf16[2048,2048]{1,0:T(8,128)(2,1)} %get-tuple-element.38.gram, bf16[64,2048]{1,0:T(8,128)(2,1)S(1)} %copy-done.2, ...), custom_call_target="tpu_custom_call" | custom-call | flops 1000000000 | bytes 10000000 | tf_op jit(solution)/shard_map/solve_finish/pallas_call | solution.py:479
  270.6 3.3 %collective-permute-start.6 = (bf16[64,2048]{1,0:T(8,128)(2,1)S(1)}, bf16[64,2048]{1,0:T(8,128)(2,1)S(1)}, u32[]{:S(2)}, u32[]{:S(2)}) collective-permute-start(bf16[64,2048]{1,0:T(8,128)(2,1)S(1)} %solve_finish.1), channel_id=1, source_target_pairs={{0,2},{2,0},{1,3},{3,1},{4,6},{6,4},{5,7},{7,5},{8,10},{10,8},{9,1... | collective-permute-start | bytes 786440 | tf_op jit(solution)/shard_map/ppermute | solution.py:583
  273.9 3.6 %convolution_multiply_fusion.3.refs_0_ = f32[64,1024]{1,0:T(8,128)S(1)} fusion(bf16[64,2048]{1,0:T(8,128)(2,1)S(1)} %solve_finish.1, bf16[1024,2048]{1,0:T(8,128)(2,1)} %all-gather.2.cloned.1.call-done), kind=kOutput, calls=%fused_computation.3 | convolution fusion | flops 268500992 | bytes 4718592 | tf_op jit(solution)/shard_map/dot_general | solution.py:589
  277.5 3.2 %collective-permute-done.6 = bf16[64,2048]{1,0:T(8,128)(2,1)S(1)} collective-permute-done((bf16[64,2048]{1,0:T(8,128)(2,1)S(1)}, bf16[64,2048]{1,0:T(8,128)(2,1)S(1)}, u32[]{:S(2)}, u32[]{:S(2)}) %collective-permute-start.6) | collective-permute-done | bytes 262176 | tf_op jit(solution)/shard_map/ppermute | solution.py:583
  283.5 3.2 %collective-permute-start.8 = (bf16[64,2048]{1,0:T(8,128)(2,1)S(1)}, bf16[64,2048]{1,0:T(8,128)(2,1)S(1)}, u32[]{:S(2)}, u32[]{:S(2)}) collective-permute-start(bf16[64,2048]{1,0:T(8,128)(2,1)S(1)} %pad_maximum_fusion), channel_id=1, source_target_pairs={{0,2},{2,0},{1,3},{3,1},{4,6},{6,4},{5,7},{7,5},{8,10},{10,8},{9,1... | collective-permute-start | bytes 786440 | tf_op jit(solution)/shard_map/ppermute | solution.py:594
  288.1 4.6 %collective-permute-done.8 = bf16[64,2048]{1,0:T(8,128)(2,1)S(1)} collective-permute-done((bf16[64,2048]{1,0:T(8,128)(2,1)S(1)}, bf16[64,2048]{1,0:T(8,128)(2,1)S(1)}, u32[]{:S(2)}, u32[]{:S(2)}) %collective-permute-start.8) | collective-permute-done | bytes 262176 | tf_op jit(solution)/shard_map/ppermute | solution.py:594
  292.7 2.2 place.1
  (52 shorter events, 16.1 us)
Async XLA Ops:
  7.1 17.5 %copy-start.11 = (s32[128]{0:T(128)S(1)}, s32[128]{0:T(128)}, u32[]{:S(2)}) copy-start(s32[128]{0:T(128)} %param.15) | copy-start | bytes 1540
  7.1 17.7 %copy-start.10 = (s32[256]{0:T(256)S(1)}, s32[256]{0:T(256)}, u32[]{:S(2)}) copy-start(s32[256]{0:T(256)} %param.14) | copy-start | bytes 3076
  18.9 54.0 %copy-start.5 = (s32[4]{0:T(128)S(1)}, s32[4]{0:T(128)}, u32[]{:S(2)}) copy-start(s32[4]{0:T(128)} %pad_add_fusion.1.at_ref.core_ref.place_ref) | copy-start | bytes 52
  19.0 2.3 collective-permute-start
  22.4 10.6 %collective-permute-start.1 = (f32[6,96,128]{2,1,0:T(8,128)S(1)}, f32[6,96,128]{2,1,0:T(8,128)S(1)}, u32[]{:S(2)}, u32[]{:S(2)}) collective-permute-start(f32[6,96,128]{2,1,0:T(8,128)S(1)} %get-tuple-element.47), channel_id=1, source_target_pairs={{0,2},{2,0},{1,3},{3,1},{4,6},{6,4},{5,7},{7,5},{8,10},{10,8},{9,1... | collective-permute-start | bytes 884744 | tf_op jit(solution)/shard_map/ppermute | solution.py:528
  33.8 1.3 copy-start
  35.1 0.7 copy-start.1
  35.8 37.2 %all-to-all-start = ((bf16[32,64,512]{2,1,0:T(8,128)(2,1)}), bf16[32,64,512]{2,1,0:T(8,128)(2,1)S(1)}, u32[]{:S(2)}, u32[]{:S(2)}) async-start(bf16[32,64,512]{2,1,0:T(8,128)(2,1)} %copy-done), calls=%async_computation | async-start | bytes 4194304 | tf_op jit(solution)/shard_map/all_to_all | solution.py:570
  45.4 224.9 %all-gather.2.cloned.1.call-start = ((), (), s32[]{:S(2)}) async-start(), calls=%async_computation.3 | async-start | bytes 4456448 | tf_op jit(solution)/shard_map/all_gather | solution.py:572
  74.2 1.4 collective-permute-start.2
  76.3 5.8 %collective-permute-start.3 = (f32[136,128]{1,0:T(8,128)S(1)}, f32[136,128]{1,0:T(8,128)S(1)}, u32[]{:S(2)}, u32[]{:S(2)}) collective-permute-start(f32[136,128]{1,0:T(8,128)S(1)} %get-tuple-element.49), channel_id=1, source_target_pairs={{0,2},{2,0},{1,3},{3,1},{4,6},{6,4},{5,7},{7,5},{8,10},{10,8},{9,1... | collective-permute-start | bytes 208904 | tf_op jit(solution)/shard_map/ppermute | solution.py:528
  85.2 38.3 %all-to-all-start.1 = ((bf16[64,136,128]{2,1,0:T(8,128)(2,1)}), bf16[64,136,128]{2,1,0:T(8,128)(2,1)}, u32[]{:S(2)}, u32[]{:S(2)}) async-start(bf16[64,136,128]{2,1,0:T(8,128)(2,1)} %split_high.1), calls=%async_computation.1 | async-start | bytes 4456448 | tf_op jit(solution)/shard_map/all_to_all | solution.py:532
  96.9 73.3 %copy-start.2 = (bf16[64,2048]{1,0:T(8,128)(2,1)S(1)}, bf16[64,2048]{1,0:T(8,128)(2,1)}, u32[]{:S(2)}) copy-start(bf16[64,2048]{1,0:T(8,128)(2,1)} %copy-done.1) | copy-start | bytes 786436
  96.9 73.3 %copy-start.6 = (s32[4]{0:T(128)S(1)}, s32[4]{0:T(128)}, u32[]{:S(2)}) copy-start(s32[4]{0:T(128)} %pad_add_fusion.1.at_ref.core_ref.place_ref) | copy-start | bytes 52
  123.5 6.0 %collective-permute-start.4 = (bf16[64,136,128]{2,1,0:T(8,128)(2,1)}, bf16[64,136,128]{2,1,0:T(8,128)(2,1)}, u32[]{:S(2)}, u32[]{:S(2)}) collective-permute-start(bf16[64,136,128]{2,1,0:T(8,128)(2,1)} %all-to-all-done.1.own), channel_id=1, source_target_pairs={{0,1},{1,0},{2,3},{3,2},{4,5},{5,4},{6,7},{7,6},{8,9},{9,8},{10,11... | collective-permute-start | bytes 6684680 | tf_op jit(solution)/shard_map/ppermute | solution.py:576
  123.5 42.3 %all-to-all-start.2 = ((bf16[64,136,128]{2,1,0:T(8,128)(2,1)}), bf16[64,136,128]{2,1,0:T(8,128)(2,1)S(1)}, u32[]{:S(2)}, u32[]{:S(2)}) async-start(bf16[64,136,128]{2,1,0:T(8,128)(2,1)} %split_low.1), calls=%async_computation.2 | async-start | bytes 4456448 | tf_op jit(solution)/shard_map/all_to_all | solution.py:532
  165.8 4.3 %collective-permute-start.5 = (bf16[64,136,128]{2,1,0:T(8,128)(2,1)S(1)}, bf16[64,136,128]{2,1,0:T(8,128)(2,1)S(1)}, u32[]{:S(2)}, u32[]{:S(2)}) collective-permute-start(bf16[64,136,128]{2,1,0:T(8,128)(2,1)S(1)} %all-to-all-done.2.own), channel_id=1, source_target_pairs={{0,1},{1,0},{2,3},{3,2},{4,5},{5,4},{6,7},{7,6},{8,9},{9,8},{10,11... | collective-permute-start | bytes 6684680 | tf_op jit(solution)/shard_map/ppermute | solution.py:580
  170.2 1.0 copy-start.3
  171.2 0.9 copy-start.4
  172.2 0.7 copy-start.7
  270.3 10.3 %copy-start.8 = (bf16[1024,2048]{1,0:T(8,128)(2,1)S(1)}, bf16[1024,2048]{1,0:T(8,128)(2,1)}, u32[]{:S(2)}) copy-start(bf16[1024,2048]{1,0:T(8,128)(2,1)} %all-gather.2.cloned.1.call-done) | copy-start | bytes 12582916
  270.3 11.7 %collective-permute-start.7 = (bf16[1024,2048]{1,0:T(8,128)(2,1)}, bf16[1024,2048]{1,0:T(8,128)(2,1)S(1)}, u32[]{:S(2)}, u32[]{:S(2)}) collective-permute-start(bf16[1024,2048]{1,0:T(8,128)(2,1)} %all-gather.2.cloned.1.call-done), channel_id=1, source_target_pairs={{0,1},{1,0},{2,3},{3,2},{4,5},{5,4},{6,7},{7,6},{8,9},{9,8},{10,11... | collective-permute-start | bytes 12582920 | tf_op jit(solution)/shard_map/ppermute | solution.py:584
  270.6 10.1 %collective-permute-start.6 = (bf16[64,2048]{1,0:T(8,128)(2,1)S(1)}, bf16[64,2048]{1,0:T(8,128)(2,1)S(1)}, u32[]{:S(2)}, u32[]{:S(2)}) collective-permute-start(bf16[64,2048]{1,0:T(8,128)(2,1)S(1)} %solve_finish.1), channel_id=1, source_target_pairs={{0,2},{2,0},{1,3},{3,1},{4,6},{6,4},{5,7},{7,5},{8,10},{10,8},{9,1... | collective-permute-start | bytes 786440 | tf_op jit(solution)/shard_map/ppermute | solution.py:583
  283.5 9.2 %collective-permute-start.8 = (bf16[64,2048]{1,0:T(8,128)(2,1)S(1)}, bf16[64,2048]{1,0:T(8,128)(2,1)S(1)}, u32[]{:S(2)}, u32[]{:S(2)}) collective-permute-start(bf16[64,2048]{1,0:T(8,128)(2,1)S(1)} %pad_maximum_fusion), channel_id=1, source_target_pairs={{0,2},{2,0},{1,3},{3,1},{4,6},{6,4},{5,7},{7,5},{8,10},{10,8},{9,1... | collective-permute-start | bytes 786440 | tf_op jit(solution)/shard_map/ppermute | solution.py:594
  (1 other events, 0.6 us)
Sparse Core Ops, SparseCore 0:
  73.1 89.8 all-gather.1

commit v2 on v1

--- a/solution.py
+++ b/solution.py
@@ -18,7 +18,8 @@
 GROUPS = K // GROUP
 EXTRA = 136
 TOL = 2.0**-9
-START_STEPS = 13
+START_STEPS = 12
+SLABS = 8
 START_FLOPS = 10**9
 FINISH_FLOPS = 10**9
 MAX_STEPS = 8192
@@ -223,6 +224,11 @@
         diag = jnp.sum(jnp.where(row == col, high, 0.0), axis=0, keepdims=True)
         tail[0:1, :] = diag[:, 0:128]
         tail[1:2, :] = diag[:, 128:256]
+        tail[2:3, :] = diag[:, 0:128]
+        tail[3:4, :] = diag[:, 128:256]
+        diag = jnp.sum(jnp.where(row == col, low, 0.0), axis=0, keepdims=True)
+        tail[4:5, :] = diag[:, 0:128]
+        tail[5:6, :] = diag[:, 128:256]
 
     def fill(ref, slot, q):
         ref[slot, 0:64, :] = block[64 * q : 64 * q + 64, 0:128]
@@ -257,9 +263,14 @@
 
 def split_kernel(want_low, mine_ref, got_ref, out_ref):
     total = mine_ref[...] + got_ref[...]
-    part = total.astype(BF16)
+    high = total.astype(BF16).astype(F32)
+    low = total - high
     if want_low:
-        part = (total - part.astype(F32)).astype(BF16)
+        part = low.astype(BF16)
+    else:
+        row = lax.broadcasted_iota(jnp.int32, total.shape, 0)
+        fine = jnp.logical_and(row >= 130, row < 134)
+        part = jnp.where(fine, low, high).astype(BF16)
     for n in range(64):
         out_ref[n] = part
 
@@ -275,19 +286,19 @@
     )(mine, got)
 
 
-def unpack(core, own, other, out, trace_ref):
+def unpack(core, own, other, out, trace_ref, fine_ref=None):
     @pl.when(core == 0)
     def _():
-        unpack_parts((own, other), out, trace_ref)
+        unpack_parts((own, other), out, trace_ref, fine_ref)
 
     @pl.when(core == 1)
     def _():
-        unpack_parts((other, own), out, trace_ref)
+        unpack_parts((other, own), out, trace_ref, fine_ref)
 
     return jnp.sum(trace_ref[0:1, :], axis=1, keepdims=True)
 
 
-def unpack_parts(parts, out, trace_ref):
+def unpack_parts(parts, out, trace_ref, fine_ref):
     row = lax.broadcasted_iota(jnp.int32, (GROUP, GROUP), 0)
     col = lax.broadcasted_iota(jnp.int32, (GROUP, GROUP), 1)
     trace = jnp.zeros((1, GROUP), F32)
@@ -310,6 +321,9 @@
             flipped = wide.T
             tail = parts[0][2 * n, 128:EXTRA, :].astype(F32)
             diag = jnp.concatenate([tail[0:1], tail[1:2]], axis=1)
+            if fine_ref is not None:
+                fine_ref[0:1, j0 : j0 + GROUP] = jnp.concatenate([tail[2:3], tail[3:4]], axis=1)
+                fine_ref[0:1, i0 : i0 + GROUP] = jnp.concatenate([tail[4:5], tail[5:6]], axis=1)
             low = jnp.where(row >= col, wide, flipped)
             high = jnp.where(row < col, wide, jnp.where(row > col, flipped, diag))
             trace += jnp.sum(jnp.where(row == col, wide, 0.0), axis=0, keepdims=True) + diag
@@ -327,19 +341,14 @@
 
 def product(high, low, p, y, gain):
     upper = [p[:, cols].astype(BF16) for cols in BLOCKS]
+    lower = [(p[:, cols] - up.astype(F32)).astype(BF16) for cols, up in zip(BLOCKS, upper)]
     left = jnp.concatenate(upper, axis=1)
-    if low is not None:
-        lower = [(p[:, cols] - up.astype(F32)).astype(BF16) for cols, up in zip(BLOCKS, upper)]
-        both = jnp.concatenate([left, jnp.concatenate(lower, axis=1)], axis=0)
+    both = jnp.concatenate([left, jnp.concatenate(lower, axis=1)], axis=0)
     total = jnp.zeros((64, GROUP), F32)
     for cols in BLOCKS:
-        if low is None:
-            main = jnp.dot(left, high[:, cols], preferred_element_type=F32)
-        else:
-            main = jnp.dot(both, high[:, cols], preferred_element_type=F32)
-            rest = jnp.dot(left, low[:, cols], preferred_element_type=F32)
-            main = main[0:64] + main[64:128] + rest
-        value = main * gain + 0.1 * p[:, cols]
+        main = jnp.dot(both, high[:, cols], preferred_element_type=F32)
+        rest = jnp.dot(left, low[:, cols], preferred_element_type=F32)
+        value = (main[0:64] + main[64:128] + rest) * gain + 0.1 * p[:, cols]
         y[:, cols] = value
         total += value * p[:, cols]
     return jnp.sum(total, axis=1, keepdims=True)
@@ -364,6 +373,37 @@
     return new, jnp.sum(xx, axis=1, keepdims=True)
 
 
+def advance_start(high, fine, x, r, p, pb, y, gain, rr, rp):
+    left = pb[...]
+    py = jnp.zeros((64, GROUP), F32)
+    for cols in BLOCKS:
+        main = jnp.dot(left, high[:, cols], preferred_element_type=F32)
+        step = p[:, cols]
+        value = main * gain + (fine[0:1, cols] * gain + 0.1) * step
+        y[:, cols] = value
+        py += value * step
+    py = jnp.sum(py, axis=1, keepdims=True)
+    alpha = jnp.where(py > 0.0, rp / jnp.where(py > 0.0, py, 1.0), 0.0)
+    new = jnp.zeros((64, GROUP), F32)
+    for cols in BLOCKS:
+        xv = x[:, cols] + alpha * p[:, cols]
+        rv = r[:, cols] - alpha * y[:, cols]
+        x[:, cols] = xv
+        r[:, cols] = rv
+        new += rv * rv
+    new = jnp.sum(new, axis=1, keepdims=True)
+    beta = new / jnp.where(rr > 0.0, rr, 1.0)
+    rp = jnp.zeros((64, GROUP), F32)
+    for cols in BLOCKS:
+        rv = r[:, cols]
+        step = (rv + beta * p[:, cols]).astype(BF16)
+        pb[:, cols] = step
+        wide = step.astype(F32)
+        p[:, cols] = wide
+        rp += rv * wide
+    return new, jnp.sum(rp, axis=1, keepdims=True)
+
+
 def scaled(f_ref):
     f = f_ref[...].astype(F32)
     top = jnp.max(jnp.abs(f), axis=1, keepdims=True)
@@ -372,25 +412,30 @@
 
 
 def start_kernel(
-    core_ref, own, other, f_ref, x0_ref, base_ref, trace_ref, gram, high, x, r, p, y, sem
+    core_ref, own, other, f_ref, x0_ref, base_ref, trace_ref, gram, high, fine, x, r, p, pb, y, sem
 ):
     f, _ = scaled(f_ref)
     r[...] = f
-    p[...] = f
+    pb[...] = f.astype(BF16)
+    p[...] = pb[...].astype(F32)
     x[...] = jnp.zeros_like(f)
-    gain = K / unpack(core_ref[0], own, other, high, trace_ref)
-    keep = pltpu.make_async_copy(high, gram, sem)
+    trace = unpack(core_ref[0], own, other, high, trace_ref, fine)
+    gain = K / (trace + jnp.sum(fine[0:1, :], axis=1, keepdims=True))
+    keep = pltpu.make_async_copy(high, gram.at[0], sem)
     keep.start()
     lax.fori_loop(
         0,
         START_STEPS,
-        lambda _, rr: advance(high, None, x, r, p, y, gain, rr)[0],
-        rows_dot(f, f),
+        lambda _, state: advance_start(high, fine, x, r, p, pb, y, gain, *state),
+        (rows_dot(f, f), rows_dot(f, p[...])),
     )
-    x0 = x[...].astype(BF16)
+    x0 = x[...]
     x0_ref[...] = x0
-    for cols in BLOCKS:
-        base_ref[:, cols] = jnp.dot(x0, high[:, cols], preferred_element_type=F32)
+    upper = x0.astype(BF16)
+    both = jnp.concatenate([upper, (x0 - upper.astype(F32)).astype(BF16)], axis=0)
+    for cols in BLOCKS:
+        main = jnp.dot(both, high[:, cols], preferred_element_type=F32)
+        base_ref[:, cols] = main[0:64] + main[64:128]
     keep.wait()
 
 
@@ -400,21 +445,23 @@
         in_specs=[pl.BlockSpec(memory_space=pltpu.SMEM)] + [vmem_spec()] * 3,
         out_specs=[vmem_spec()] * 3 + [pl.BlockSpec(memory_space=pl.ANY)],
         out_shape=[
-            jax.ShapeDtypeStruct((64, K), BF16),
+            jax.ShapeDtypeStruct((64, K), F32),
             jax.ShapeDtypeStruct((64, K), F32),
             jax.ShapeDtypeStruct((8, GROUP), F32),
-            jax.ShapeDtypeStruct((K, K), BF16),
+            jax.ShapeDtypeStruct((SLABS, K, K), BF16),
         ],
         scratch_shapes=[
             pltpu.VMEM((K, K), BF16),
-            pltpu.VMEM((64, K), F32),
-            pltpu.VMEM((64, K), F32),
-            pltpu.VMEM((64, K), F32),
+            pltpu.VMEM((8, K), F32),
+            pltpu.VMEM((64, K), F32),
+            pltpu.VMEM((64, K), F32),
+            pltpu.VMEM((64, K), F32),
+            pltpu.VMEM((64, K), BF16),
             pltpu.VMEM((64, K), F32),
             pltpu.SemaphoreType.DMA,
         ],
         cost_estimate=pl.CostEstimate(flops=START_FLOPS, bytes_accessed=10**7, transcendentals=0),
-        compiler_params=params(60),
+        compiler_params=params(18),
         name="solve_start",
     )(core, own, other, f)
 
@@ -438,22 +485,23 @@
     y,
     sem,
 ):
-    load = pltpu.make_async_copy(gram, high, sem)
+    load = pltpu.make_async_copy(gram.at[0], high, sem)
     load.start()
     f, top = scaled(f_ref)
     trace = jnp.sum(trace_ref[0:1, :], axis=1, keepdims=True)
     trace = trace + unpack(core_ref[0], own, other, low, low_trace)
     gain = K / trace
     x0 = x0_ref[...]
-    for cols in BLOCKS:
-        main = base_ref[:, cols] + jnp.dot(x0, low[:, cols], preferred_element_type=F32)
-        y[:, cols] = main * gain + 0.1 * x0_ref[:, cols].astype(F32)
+    upper = x0.astype(BF16)
+    for cols in BLOCKS:
+        main = base_ref[:, cols] + jnp.dot(upper, low[:, cols], preferred_element_type=F32)
+        y[:, cols] = main * gain + 0.1 * x0_ref[:, cols]
     ff = rows_dot(f, f)
     rest = f - y[...]
     rr = rows_dot(rest, rest)
     good = rr <= ff
     rr = jnp.where(good, rr, ff)
-    first = jnp.where(good, x0.astype(F32), 0.0)
+    first = jnp.where(good, x0, 0.0)
     rest = jnp.where(good, rest, f)
     x[...] = first
     r[...] = rest
@@ -494,7 +542,7 @@
             pltpu.SemaphoreType.DMA,
         ],
         cost_estimate=pl.CostEstimate(flops=FINISH_FLOPS, bytes_accessed=10**7, transcendentals=0),
-        compiler_params=params(46),
+        compiler_params=params(28),
         name="solve_finish",
     )(core, own, other, high, f, x0, base, trace)
 

time: 304 us -> 302 us (level)
  waiting for transfers between devices: 61.9 us -> 68.3 us
  starting transfers between devices: 36.1 us -> 30.1 us
  transfers between devices with their start and end apart: 13 -> 13, of which waited for: 10 -> 10; matrix products, arithmetic and copies ran while one was open for 2% -> 3% of each run, Pallas kernels for 44% -> 44%
where the time goes in v2:
time: 302 us; the launch traced here: 300 us
  Pallas kernels  148 us (49%)
  waiting for transfers between devices  68.3 us (23%)
  starting transfers between devices  30.1 us (10%)
  blocking collectives  25.5 us (8%)
  between operations  13.6 us (5%)
  matrix products  7.97 us (3%)
  local copies, waits for them, and re-layouts  4.18 us (1%)
    pallas_call x1, Pallas kernels, solve_finish(): pl.pallas_call(finish_kernel, in_specs=[pl.BlockSpec(memory_space=pltpu.S...  97.5 us
    all_to_all x2, waiting for transfers between devices, exchange(): lax.all_to_all(chunks, ('dp', 'proj'), 0, 0, axis_index_groups=SAME_CORE,...  33 us
    pallas_call x1, Pallas kernels, solve_start(): pl.pallas_call(start_kernel, in_specs=[pl.BlockSpec(memory_space=pltpu.SM...  29.1 us
    all_gather x1, blocking collectives, per_device(): lax.all_gather(test, 'dp', axis_index_groups=NEAR, axis=0, tiled=True)  25.5 us
    all_to_all x2, starting transfers between devices, exchange(): lax.all_to_all(chunks, ('dp', 'proj'), 0, 0, axis_index_groups=SAME_CORE,...  15.2 us
    pallas_call x1, Pallas kernels, project(): pl.pallas_call(project_kernel, in_specs=[pl.BlockSpec(memory_space=pltpu....  11.9 us
    ppermute x2, waiting for transfers between devices, fold(): lax.ppermute(keep[1] + recv[1], 'proj', FAR_SWAP)  11.7 us
    all_to_all x1, starting transfers between devices, per_device(): rows = lax.all_to_all(send, 'dp', 0, 0, tiled=True).reshape(2048, 2 * GROUP)  9.57 us
  transfers between devices with their start and end apart: 13, of which 10 were waited for; matrix products, arithmetic and copies ran while one was open for 3% of the time, Pallas kernels for 44%

profile of v2, /device:TPU:2, one launch (start us, length us, event | category | flops | bytes accessed | tf_op | source)
XLA Modules:
  0.0 299.6 jit_solution(2202128478644696569)
XLA Ops:
  7.1 11.9 %project.1 = (f32[2,6,96,128]{3,2,1,0:T(8,128)}, f32[2,6,96,128]{3,2,1,0:T(8,128)}) custom-call(s32[4]{0:T(128)} %pad_add_fusion.1.at_ref.core_ref.place_ref, bf16[8,2752,256]{2,1,0:T(8,128)(2,1)} %bitcast.27, bf16[8,2752,128]{2,1,0:T(8,128)(2,1)} %bitcast.28, bf16[2048,1024]{1,0:T(8,128)(2,1)} %bitcast.29, bf16[1024,1024]{1,0:T(8,128)(2,1)} %bitcast.30, ...), custom_call_target="tpu_custom_call" | custom-call | flops 1000000000 | bytes 30000000 | tf_op jit(solution)/shard_map/project/pallas_call | solution.py:137
  19.1 2.2 collective-permute-done
  22.5 2.2 collective-permute-start.1
  25.0 8.1 %collective-permute-done.1.got_ref = f32[6,96,128]{2,1,0:T(8,128)S(1)} collective-permute-done((f32[6,96,128]{2,1,0:T(8,128)S(1)}, f32[6,96,128]{2,1,0:T(8,128)S(1)}, u32[]{:S(2)}, u32[]{:S(2)}) %collective-permute-start.1) | collective-permute-done | bytes 294944 | tf_op jit(solution)/shard_map/ppermute | solution.py:576
  35.2 9.6 %all-to-all-start = ((bf16[32,64,512]{2,1,0:T(8,128)(2,1)}), bf16[32,64,512]{2,1,0:T(8,128)(2,1)S(1)}, u32[]{:S(2)}, u32[]{:S(2)}) async-start(bf16[32,64,512]{2,1,0:T(8,128)(2,1)} %copy-done), calls=%async_computation | async-start | bytes 4194304 | tf_op jit(solution)/shard_map/all_to_all | solution.py:618
  44.8 25.5 %all_gather.6 = bf16[64,2048]{1,0:T(8,128)(2,1)} all-gather(bf16[32,2048]{1,0:T(8,128)(2,1)S(1)} %get-tuple-element.29), channel_id=1, replica_groups={{0,64},{4,68},{8,72},{12,76},{16,80},{20,84},{24,88},{28,92},{32,96},{3..., dimensions={0}, use_global_device_ids=true | all-gather | bytes 393216 | tf_op jit(solution)/shard_map/all_gather | solution.py:617
  70.3 2.1 all-to-all-done
  75.7 2.1 collective-permute-start.3
  77.9 3.7 %collective-permute-done.3.got_ref = f32[136,128]{1,0:T(8,128)S(1)} collective-permute-done((f32[136,128]{1,0:T(8,128)S(1)}, f32[136,128]{1,0:T(8,128)S(1)}, u32[]{:S(2)}, u32[]{:S(2)}) %collective-permute-start.3) | collective-permute-done | bytes 69664 | tf_op jit(solution)/shard_map/ppermute | solution.py:576
  82.2 2.5 split_high.1
  84.7 9.3 %all-to-all-start.1 = ((bf16[64,136,128]{2,1,0:T(8,128)(2,1)}), bf16[64,136,128]{2,1,0:T(8,128)(2,1)}, u32[]{:S(2)}, u32[]{:S(2)}) async-start(bf16[64,136,128]{2,1,0:T(8,128)(2,1)} %split_high.1), calls=%async_computation.1 | async-start | bytes 4456448 | tf_op jit(solution)/shard_map/all_to_all | solution.py:580
  93.9 2.5 split_low.1
  96.4 26.5 %all-to-all-done.1.own = bf16[64,136,128]{2,1,0:T(8,128)(2,1)} async-done(((bf16[64,136,128]{2,1,0:T(8,128)(2,1)}), bf16[64,136,128]{2,1,0:T(8,128)(2,1)}, u32[]{:S(2)}, u32[]{:S(2)}) %all-to-all-start.1) | async-done | bytes 2228256 | tf_op jit(solution)/shard_map/all_to_all | solution.py:580
  122.9 5.9 %all-to-all-start.2 = ((bf16[64,136,128]{2,1,0:T(8,128)(2,1)}), bf16[64,136,128]{2,1,0:T(8,128)(2,1)S(1)}, u32[]{:S(2)}, u32[]{:S(2)}) async-start(bf16[64,136,128]{2,1,0:T(8,128)(2,1)} %split_low.1), calls=%async_computation.2 | async-start | bytes 4456448 | tf_op jit(solution)/shard_map/all_to_all | solution.py:580
  128.9 29.1 %solve_start.1 = (f32[64,2048]{1,0:T(8,128)S(1)}, f32[64,2048]{1,0:T(8,128)S(1)}, f32[8,256]{1,0:T(8,128)S(1)}, bf16[8,2048,2048]{2,1,0:T(8,128)(2,1)}) custom-call(s32[4]{0:T(128)S(1)} %copy-done.3, bf16[64,136,128]{2,1,0:T(8,128)(2,1)} %all-to-all-done.1.own, bf16[64,136,128]{2,1,0:T(8,128)(2,1)} %collective-permute-done.4.other, ...), custom_call_target="tpu_custom_call" | custom-call | flops 1000000000 | bytes 10000000 | tf_op jit(solution)/shard_map/solve_start/pallas_call | solution.py:443
  158.8 6.5 %all-to-all-done.2.own = bf16[64,136,128]{2,1,0:T(8,128)(2,1)S(1)} async-done(((bf16[64,136,128]{2,1,0:T(8,128)(2,1)}), bf16[64,136,128]{2,1,0:T(8,128)(2,1)S(1)}, u32[]{:S(2)}, u32[]{:S(2)}) %all-to-all-start.2) | async-done | bytes 2228256 | tf_op jit(solution)/shard_map/all_to_all | solution.py:580
  165.3 4.3 %collective-permute-done.5.other = bf16[64,136,128]{2,1,0:T(8,128)(2,1)S(1)} collective-permute-done((bf16[64,136,128]{2,1,0:T(8,128)(2,1)S(1)}, bf16[64,136,128]{2,1,0:T(8,128)(2,1)S(1)}, u32[]{:S(2)}, u32[]{:S(2)}) %collective-permute-start.5) | collective-permute-done | bytes 2228256 | tf_op jit(solution)/shard_map/ppermute | solution.py:628
  170.6 97.5 %solve_finish.1 = bf16[64,2048]{1,0:T(8,128)(2,1)S(1)} custom-call(s32[4]{0:T(128)S(1)} %copy-done.3, bf16[64,136,128]{2,1,0:T(8,128)(2,1)S(1)} %all-to-all-done.2.own, bf16[64,136,128]{2,1,0:T(8,128)(2,1)S(1)} %collective-permute-done.5.other, bf16[8,2048,2048]{2,1,0:T(8,128)(2,1)} %get-tuple-element.38.gram, bf16[64,2048]{1,0:T(8,128)(2,1)S(1)} %get-tuple-element.35.f_ref, ...), custom_call_target="tpu_custom_call" | custom-call | flops 1000000000 | bytes 10000000 | tf_op jit(solution)/shard_map/solve_finish/pallas_call | solution.py:527
  268.6 3.8 %convolution_multiply_fusion.3.refs_0_ = f32[64,1024]{1,0:T(8,128)S(1)} fusion(bf16[64,2048]{1,0:T(8,128)(2,1)S(1)} %solve_finish.1, bf16[1024,2048]{1,0:T(8,128)(2,1)} %all-gather.2.cloned.1.call-done), kind=kOutput, calls=%fused_computation.3 | convolution fusion | flops 268500992 | bytes 4718592 | tf_op jit(solution)/shard_map/dot_general | solution.py:637
  272.4 6.1 %collective-permute-done.6 = bf16[64,2048]{1,0:T(8,128)(2,1)S(1)} collective-permute-done((bf16[64,2048]{1,0:T(8,128)(2,1)S(1)}, bf16[64,2048]{1,0:T(8,128)(2,1)S(1)}, u32[]{:S(2)}, u32[]{:S(2)}) %collective-permute-start.6) | collective-permute-done | bytes 262176 | tf_op jit(solution)/shard_map/ppermute | solution.py:631
  279.9 1.4 fusion.1
  281.7 1.4 convolution_multiply_fusion.2.refs_1_
  283.1 7.4 %collective-permute-done.8 = bf16[64,2048]{1,0:T(8,128)(2,1)S(1)} collective-permute-done((bf16[64,2048]{1,0:T(8,128)(2,1)S(1)}, bf16[64,2048]{1,0:T(8,128)(2,1)S(1)}, u32[]{:S(2)}, u32[]{:S(2)}) %collective-permute-start.8) | collective-permute-done | bytes 262176 | tf_op jit(solution)/shard_map/ppermute | solution.py:642
  290.5 2.2 place.1
  (44 shorter events, 12.4 us)
Async XLA Ops:
  7.1 17.5 %copy-start.7 = (s32[128]{0:T(128)S(1)}, s32[128]{0:T(128)}, u32[]{:S(2)}) copy-start(s32[128]{0:T(128)} %param.15) | copy-start | bytes 1540
  7.1 17.7 %copy-start.6 = (s32[256]{0:T(256)S(1)}, s32[256]{0:T(256)}, u32[]{:S(2)}) copy-start(s32[256]{0:T(256)} %param.14) | copy-start | bytes 3076
  19.0 53.4 %copy-start.3 = (s32[4]{0:T(128)S(1)}, s32[4]{0:T(128)}, u32[]{:S(2)}) copy-start(s32[4]{0:T(128)} %pad_add_fusion.1.at_ref.core_ref.place_ref) | copy-start | bytes 52
  19.0 2.3 collective-permute-start
  22.5 10.6 %collective-permute-start.1 = (f32[6,96,128]{2,1,0:T(8,128)S(1)}, f32[6,96,128]{2,1,0:T(8,128)S(1)}, u32[]{:S(2)}, u32[]{:S(2)}) collective-permute-start(f32[6,96,128]{2,1,0:T(8,128)S(1)} %get-tuple-element.47), channel_id=1, source_target_pairs={{0,2},{2,0},{1,3},{3,1},{4,6},{6,4},{5,7},{7,5},{8,10},{10,8},{9,1... | collective-permute-start | bytes 884744 | tf_op jit(solution)/shard_map/ppermute | solution.py:576
  33.9 1.4 copy-start
  35.2 37.1 %all-to-all-start = ((bf16[32,64,512]{2,1,0:T(8,128)(2,1)}), bf16[32,64,512]{2,1,0:T(8,128)(2,1)S(1)}, u32[]{:S(2)}, u32[]{:S(2)}) async-start(bf16[32,64,512]{2,1,0:T(8,128)(2,1)} %copy-done), calls=%async_computation | async-start | bytes 4194304 | tf_op jit(solution)/shard_map/all_to_all | solution.py:618
  44.8 223.4 %all-gather.2.cloned.1.call-start = ((), (), s32[]{:S(2)}) async-start(), calls=%async_computation.3 | async-start | bytes 4456448 | tf_op jit(solution)/shard_map/all_gather | solution.py:620
  73.7 1.4 collective-permute-start.2
  75.7 5.8 %collective-permute-start.3 = (f32[136,128]{1,0:T(8,128)S(1)}, f32[136,128]{1,0:T(8,128)S(1)}, u32[]{:S(2)}, u32[]{:S(2)}) collective-permute-start(f32[136,128]{1,0:T(8,128)S(1)} %get-tuple-element.49), channel_id=1, source_target_pairs={{0,2},{2,0},{1,3},{3,1},{4,6},{6,4},{5,7},{7,5},{8,10},{10,8},{9,1... | collective-permute-start | bytes 208904 | tf_op jit(solution)/shard_map/ppermute | solution.py:576
  81.6 0.6 copy-start.5
  84.7 38.3 %all-to-all-start.1 = ((bf16[64,136,128]{2,1,0:T(8,128)(2,1)}), bf16[64,136,128]{2,1,0:T(8,128)(2,1)}, u32[]{:S(2)}, u32[]{:S(2)}) async-start(bf16[64,136,128]{2,1,0:T(8,128)(2,1)} %split_high.1), calls=%async_computation.1 | async-start | bytes 4456448 | tf_op jit(solution)/shard_map/all_to_all | solution.py:580
  122.9 6.0 %collective-permute-start.4 = (bf16[64,136,128]{2,1,0:T(8,128)(2,1)}, bf16[64,136,128]{2,1,0:T(8,128)(2,1)}, u32[]{:S(2)}, u32[]{:S(2)}) collective-permute-start(bf16[64,136,128]{2,1,0:T(8,128)(2,1)} %all-to-all-done.1.own), channel_id=1, source_target_pairs={{0,1},{1,0},{2,3},{3,2},{4,5},{5,4},{6,7},{7,6},{8,9},{9,8},{10,11... | collective-permute-start | bytes 6684680 | tf_op jit(solution)/shard_map/ppermute | solution.py:624
  122.9 42.3 %all-to-all-start.2 = ((bf16[64,136,128]{2,1,0:T(8,128)(2,1)}), bf16[64,136,128]{2,1,0:T(8,128)(2,1)S(1)}, u32[]{:S(2)}, u32[]{:S(2)}) async-start(bf16[64,136,128]{2,1,0:T(8,128)(2,1)} %split_low.1), calls=%async_computation.2 | async-start | bytes 4456448 | tf_op jit(solution)/shard_map/all_to_all | solution.py:580
  158.0 0.8 copy-start.1
  165.3 4.3 %collective-permute-start.5 = (bf16[64,136,128]{2,1,0:T(8,128)(2,1)S(1)}, bf16[64,136,128]{2,1,0:T(8,128)(2,1)S(1)}, u32[]{:S(2)}, u32[]{:S(2)}) collective-permute-start(bf16[64,136,128]{2,1,0:T(8,128)(2,1)S(1)} %all-to-all-done.2.own), channel_id=1, source_target_pairs={{0,1},{1,0},{2,3},{3,2},{4,5},{5,4},{6,7},{7,6},{8,9},{9,8},{10,11... | collective-permute-start | bytes 6684680 | tf_op jit(solution)/shard_map/ppermute | solution.py:628
  169.6 1.0 copy-start.2
  268.2 10.3 %copy-start.4 = (bf16[1024,2048]{1,0:T(8,128)(2,1)S(1)}, bf16[1024,2048]{1,0:T(8,128)(2,1)}, u32[]{:S(2)}) copy-start(bf16[1024,2048]{1,0:T(8,128)(2,1)} %all-gather.2.cloned.1.call-done) | copy-start | bytes 12582916
  268.2 11.7 %collective-permute-start.7 = (bf16[1024,2048]{1,0:T(8,128)(2,1)}, bf16[1024,2048]{1,0:T(8,128)(2,1)S(1)}, u32[]{:S(2)}, u32[]{:S(2)}) collective-permute-start(bf16[1024,2048]{1,0:T(8,128)(2,1)} %all-gather.2.cloned.1.call-done), channel_id=1, source_target_pairs={{0,1},{1,0},{2,3},{3,2},{4,5},{5,4},{6,7},{7,6},{8,9},{9,8},{10,11... | collective-permute-start | bytes 12582920 | tf_op jit(solution)/shard_map/ppermute | solution.py:632
  268.3 10.2 %collective-permute-start.6 = (bf16[64,2048]{1,0:T(8,128)(2,1)S(1)}, bf16[64,2048]{1,0:T(8,128)(2,1)S(1)}, u32[]{:S(2)}, u32[]{:S(2)}) collective-permute-start(bf16[64,2048]{1,0:T(8,128)(2,1)S(1)} %solve_finish.1), channel_id=1, source_target_pairs={{0,2},{2,0},{1,3},{3,1},{4,6},{6,4},{5,7},{7,5},{8,10},{10,8},{9,1... | collective-permute-start | bytes 786440 | tf_op jit(solution)/shard_map/ppermute | solution.py:631
  281.3 9.2 %collective-permute-start.8 = (bf16[64,2048]{1,0:T(8,128)(2,1)S(1)}, bf16[64,2048]{1,0:T(8,128)(2,1)S(1)}, u32[]{:S(2)}, u32[]{:S(2)}) collective-permute-start(bf16[64,2048]{1,0:T(8,128)(2,1)S(1)} %pad_maximum_fusion), channel_id=1, source_target_pairs={{0,2},{2,0},{1,3},{3,1},{4,6},{6,4},{5,7},{7,5},{8,10},{10,8},{9,1... | collective-permute-start | bytes 786440 | tf_op jit(solution)/shard_map/ppermute | solution.py:642
Sparse Core Ops, SparseCore 0:
  72.5 89.8 all-gather.1

commit v3 on v2

--- a/solution.py
+++ b/solution.py
@@ -18,7 +18,7 @@
 GROUPS = K // GROUP
 EXTRA = 136
 TOL = 2.0**-9
-START_STEPS = 12
+START_STEPS = 13
 SLABS = 8
 START_FLOPS = 10**9
 FINISH_FLOPS = 10**9

time: 302 us -> 296 us (0.980); the launches traced: 300 us -> 290 us
  Pallas kernels: 148 us -> 134 us
  starting transfers between devices: 30.1 us -> 36.1 us
    pallas_call x1, Pallas kernels: 97.5 us -> 82 us  [solve_finish(): pl.pallas_call(finish_kernel, in_specs=[pl.BlockSpec(memory_space=pltpu.S...]
    ppermute x1, starting transfers between devices: 0.08 us -> 6.43 us  [per_device(): tests_other = lax.ppermute(tests, 'proj', CORE_SWAP)]
  transfers between devices with their start and end apart: 13 -> 13, of which waited for: 10 -> 10; matrix products, arithmetic and copies ran while one was open for 3% -> 3% of each run, Pallas kernels for 44% -> 41%
where the time goes in v3:
time: 296 us; the launch traced here: 290 us
  Pallas kernels  134 us (45%)
  waiting for transfers between devices  66.8 us (23%)
  starting transfers between devices  36.1 us (12%)
  blocking collectives  25.5 us (9%)
  between operations  13.6 us (5%)
  matrix products  7.77 us (3%)
  local copies, waits for them, and re-layouts  4.18 us (1%)
    pallas_call x1, Pallas kernels, solve_finish(): pl.pallas_call(finish_kernel, in_specs=[pl.BlockSpec(memory_space=pltpu.S...  82 us
    all_to_all x2, waiting for transfers between devices, exchange(): lax.all_to_all(chunks, ('dp', 'proj'), 0, 0, axis_index_groups=SAME_CORE,...  31 us
    pallas_call x1, Pallas kernels, solve_start(): pl.pallas_call(start_kernel, in_specs=[pl.BlockSpec(memory_space=pltpu.SM...  31 us
    all_gather x1, blocking collectives, per_device(): lax.all_gather(test, 'dp', axis_index_groups=NEAR, axis=0, tiled=True)  25.5 us
    all_to_all x2, starting transfers between devices, exchange(): lax.all_to_all(chunks, ('dp', 'proj'), 0, 0, axis_index_groups=SAME_CORE,...  15.2 us
    pallas_call x1, Pallas kernels, project(): pl.pallas_call(project_kernel, in_specs=[pl.BlockSpec(memory_space=pltpu....  11.9 us
    ppermute x2, waiting for transfers between devices, fold(): lax.ppermute(keep[1] + recv[1], 'proj', FAR_SWAP)  11.7 us
    all_to_all x1, starting transfers between devices, per_device(): rows = lax.all_to_all(send, 'dp', 0, 0, tiled=True).reshape(2048, 2 * GROUP)  9.57 us
  transfers between devices with their start and end apart: 13, of which 10 were waited for; matrix products, arithmetic and copies ran while one was open for 3% of the time, Pallas kernels for 41%

profile of v3, /device:TPU:2, one launch (start us, length us, event | category | flops | bytes accessed | tf_op | source)
XLA Modules:
  0.0 290.3 jit_solution(17338326034082338928)
XLA Ops:
  7.1 11.9 %project.1 = (f32[2,6,96,128]{3,2,1,0:T(8,128)}, f32[2,6,96,128]{3,2,1,0:T(8,128)}) custom-call(s32[4]{0:T(128)} %pad_add_fusion.1.at_ref.core_ref.place_ref, bf16[8,2752,256]{2,1,0:T(8,128)(2,1)} %bitcast.27, bf16[8,2752,128]{2,1,0:T(8,128)(2,1)} %bitcast.28, bf16[2048,1024]{1,0:T(8,128)(2,1)} %bitcast.29, bf16[1024,1024]{1,0:T(8,128)(2,1)} %bitcast.30, ...), custom_call_target="tpu_custom_call" | custom-call | flops 1000000000 | bytes 30000000 | tf_op jit(solution)/shard_map/project/pallas_call | solution.py:137
  19.1 2.2 collective-permute-done
  22.5 2.2 collective-permute-start.1
  25.0 8.1 %collective-permute-done.1.got_ref = f32[6,96,128]{2,1,0:T(8,128)S(1)} collective-permute-done((f32[6,96,128]{2,1,0:T(8,128)S(1)}, f32[6,96,128]{2,1,0:T(8,128)S(1)}, u32[]{:S(2)}, u32[]{:S(2)}) %collective-permute-start.1) | collective-permute-done | bytes 294944 | tf_op jit(solution)/shard_map/ppermute | solution.py:576
  35.2 9.6 %all-to-all-start = ((bf16[32,64,512]{2,1,0:T(8,128)(2,1)}), bf16[32,64,512]{2,1,0:T(8,128)(2,1)S(1)}, u32[]{:S(2)}, u32[]{:S(2)}) async-start(bf16[32,64,512]{2,1,0:T(8,128)(2,1)} %copy-done), calls=%async_computation | async-start | bytes 4194304 | tf_op jit(solution)/shard_map/all_to_all | solution.py:618
  44.8 25.5 %all_gather.6 = bf16[64,2048]{1,0:T(8,128)(2,1)} all-gather(bf16[32,2048]{1,0:T(8,128)(2,1)S(1)} %get-tuple-element.29), channel_id=1, replica_groups={{0,64},{4,68},{8,72},{12,76},{16,80},{20,84},{24,88},{28,92},{32,96},{3..., dimensions={0}, use_global_device_ids=true | all-gather | bytes 393216 | tf_op jit(solution)/shard_map/all_gather | solution.py:617
  70.3 2.1 all-to-all-done
  75.7 2.1 collective-permute-start.3
  77.9 3.7 %collective-permute-done.3.got_ref = f32[136,128]{1,0:T(8,128)S(1)} collective-permute-done((f32[136,128]{1,0:T(8,128)S(1)}, f32[136,128]{1,0:T(8,128)S(1)}, u32[]{:S(2)}, u32[]{:S(2)}) %collective-permute-start.3) | collective-permute-done | bytes 69664 | tf_op jit(solution)/shard_map/ppermute | solution.py:576
  82.2 2.5 split_high.1
  84.7 9.3 %all-to-all-start.1 = ((bf16[64,136,128]{2,1,0:T(8,128)(2,1)}), bf16[64,136,128]{2,1,0:T(8,128)(2,1)}, u32[]{:S(2)}, u32[]{:S(2)}) async-start(bf16[64,136,128]{2,1,0:T(8,128)(2,1)} %split_high.1), calls=%async_computation.1 | async-start | bytes 4456448 | tf_op jit(solution)/shard_map/all_to_all | solution.py:580
  93.9 2.5 split_low.1
  96.4 26.5 %all-to-all-done.1.own = bf16[64,136,128]{2,1,0:T(8,128)(2,1)} async-done(((bf16[64,136,128]{2,1,0:T(8,128)(2,1)}), bf16[64,136,128]{2,1,0:T(8,128)(2,1)}, u32[]{:S(2)}, u32[]{:S(2)}) %all-to-all-start.1) | async-done | bytes 2228256 | tf_op jit(solution)/shard_map/all_to_all | solution.py:580
  122.9 5.9 %all-to-all-start.2 = ((bf16[64,136,128]{2,1,0:T(8,128)(2,1)}), bf16[64,136,128]{2,1,0:T(8,128)(2,1)S(1)}, u32[]{:S(2)}, u32[]{:S(2)}) async-start(bf16[64,136,128]{2,1,0:T(8,128)(2,1)} %split_low.1), calls=%async_computation.2 | async-start | bytes 4456448 | tf_op jit(solution)/shard_map/all_to_all | solution.py:580
  128.9 31.0 %solve_start.1 = (f32[64,2048]{1,0:T(8,128)S(1)}, f32[64,2048]{1,0:T(8,128)S(1)}, f32[8,256]{1,0:T(8,128)S(1)}, bf16[8,2048,2048]{2,1,0:T(8,128)(2,1)}) custom-call(s32[4]{0:T(128)S(1)} %copy-done.3, bf16[64,136,128]{2,1,0:T(8,128)(2,1)} %all-to-all-done.1.own, bf16[64,136,128]{2,1,0:T(8,128)(2,1)} %collective-permute-done.4.other, ...), custom_call_target="tpu_custom_call" | custom-call | flops 1000000000 | bytes 10000000 | tf_op jit(solution)/shard_map/solve_start/pallas_call | solution.py:443
  160.7 4.5 %all-to-all-done.2.own = bf16[64,136,128]{2,1,0:T(8,128)(2,1)S(1)} async-done(((bf16[64,136,128]{2,1,0:T(8,128)(2,1)}), bf16[64,136,128]{2,1,0:T(8,128)(2,1)S(1)}, u32[]{:S(2)}, u32[]{:S(2)}) %all-to-all-start.2) | async-done | bytes 2228256 | tf_op jit(solution)/shard_map/all_to_all | solution.py:580
  165.3 4.3 %collective-permute-done.5.other = bf16[64,136,128]{2,1,0:T(8,128)(2,1)S(1)} collective-permute-done((bf16[64,136,128]{2,1,0:T(8,128)(2,1)S(1)}, bf16[64,136,128]{2,1,0:T(8,128)(2,1)S(1)}, u32[]{:S(2)}, u32[]{:S(2)}) %collective-permute-start.5) | collective-permute-done | bytes 2228256 | tf_op jit(solution)/shard_map/ppermute | solution.py:628
  170.6 82.0 %solve_finish.1 = bf16[64,2048]{1,0:T(8,128)(2,1)S(1)} custom-call(s32[4]{0:T(128)S(1)} %copy-done.3, bf16[64,136,128]{2,1,0:T(8,128)(2,1)S(1)} %all-to-all-done.2.own, bf16[64,136,128]{2,1,0:T(8,128)(2,1)S(1)} %collective-permute-done.5.other, bf16[8,2048,2048]{2,1,0:T(8,128)(2,1)} %get-tuple-element.38.gram, bf16[64,2048]{1,0:T(8,128)(2,1)S(1)} %get-tuple-element.35.f_ref, ...), custom_call_target="tpu_custom_call" | custom-call | flops 1000000000 | bytes 10000000 | tf_op jit(solution)/shard_map/solve_finish/pallas_call | solution.py:527
  252.6 6.4 %collective-permute-start.7 = (bf16[1024,2048]{1,0:T(8,128)(2,1)}, bf16[1024,2048]{1,0:T(8,128)(2,1)S(1)}, u32[]{:S(2)}, u32[]{:S(2)}) collective-permute-start(bf16[1024,2048]{1,0:T(8,128)(2,1)} %all-gather.2.cloned.1.call-done), channel_id=1, source_target_pairs={{0,1},{1,0},{2,3},{3,2},{4,5},{5,4},{6,7},{7,6},{8,9},{9,8},{10,11... | collective-permute-start | bytes 12582920 | tf_op jit(solution)/shard_map/ppermute | solution.py:632
  259.1 3.6 %convolution_multiply_fusion.3.refs_0_ = f32[64,1024]{1,0:T(8,128)S(1)} fusion(bf16[64,2048]{1,0:T(8,128)(2,1)S(1)} %solve_finish.1, bf16[1024,2048]{1,0:T(8,128)(2,1)} %all-gather.2.cloned.1.call-done), kind=kOutput, calls=%fused_computation.3 | convolution fusion | flops 268500992 | bytes 4718592 | tf_op jit(solution)/shard_map/dot_general | solution.py:637
  262.7 6.4 %collective-permute-done.6 = bf16[64,2048]{1,0:T(8,128)(2,1)S(1)} collective-permute-done((bf16[64,2048]{1,0:T(8,128)(2,1)S(1)}, bf16[64,2048]{1,0:T(8,128)(2,1)S(1)}, u32[]{:S(2)}, u32[]{:S(2)}) %collective-permute-start.6) | collective-permute-done | bytes 262176 | tf_op jit(solution)/shard_map/ppermute | solution.py:631
  270.5 1.4 fusion.1
  273.7 7.5 %collective-permute-done.8 = bf16[64,2048]{1,0:T(8,128)(2,1)S(1)} collective-permute-done((bf16[64,2048]{1,0:T(8,128)(2,1)S(1)}, bf16[64,2048]{1,0:T(8,128)(2,1)S(1)}, u32[]{:S(2)}, u32[]{:S(2)}) %collective-permute-start.8) | collective-permute-done | bytes 262176 | tf_op jit(solution)/shard_map/ppermute | solution.py:642
  281.3 2.2 place.1
  (44 shorter events, 13.4 us)
Async XLA Ops:
  7.1 17.5 %copy-start.7 = (s32[128]{0:T(128)S(1)}, s32[128]{0:T(128)}, u32[]{:S(2)}) copy-start(s32[128]{0:T(128)} %param.15) | copy-start | bytes 1540
  7.1 17.7 %copy-start.6 = (s32[256]{0:T(256)S(1)}, s32[256]{0:T(256)}, u32[]{:S(2)}) copy-start(s32[256]{0:T(256)} %param.14) | copy-start | bytes 3076
  19.0 53.4 %copy-start.3 = (s32[4]{0:T(128)S(1)}, s32[4]{0:T(128)}, u32[]{:S(2)}) copy-start(s32[4]{0:T(128)} %pad_add_fusion.1.at_ref.core_ref.place_ref) | copy-start | bytes 52
  19.0 2.3 collective-permute-start
  22.5 10.6 %collective-permute-start.1 = (f32[6,96,128]{2,1,0:T(8,128)S(1)}, f32[6,96,128]{2,1,0:T(8,128)S(1)}, u32[]{:S(2)}, u32[]{:S(2)}) collective-permute-start(f32[6,96,128]{2,1,0:T(8,128)S(1)} %get-tuple-element.47), channel_id=1, source_target_pairs={{0,2},{2,0},{1,3},{3,1},{4,6},{6,4},{5,7},{7,5},{8,10},{10,8},{9,1... | collective-permute-start | bytes 884744 | tf_op jit(solution)/shard_map/ppermute | solution.py:576
  33.9 1.4 copy-start
  35.2 37.1 %all-to-all-start = ((bf16[32,64,512]{2,1,0:T(8,128)(2,1)}), bf16[32,64,512]{2,1,0:T(8,128)(2,1)S(1)}, u32[]{:S(2)}, u32[]{:S(2)}) async-start(bf16[32,64,512]{2,1,0:T(8,128)(2,1)} %copy-done), calls=%async_computation | async-start | bytes 4194304 | tf_op jit(solution)/shard_map/all_to_all | solution.py:618
  44.8 207.8 %all-gather.2.cloned.1.call-start = ((), (), s32[]{:S(2)}) async-start(), calls=%async_computation.3 | async-start | bytes 4456448 | tf_op jit(solution)/shard_map/all_gather | solution.py:620
  73.7 1.4 collective-permute-start.2
  75.7 5.8 %collective-permute-start.3 = (f32[136,128]{1,0:T(8,128)S(1)}, f32[136,128]{1,0:T(8,128)S(1)}, u32[]{:S(2)}, u32[]{:S(2)}) collective-permute-start(f32[136,128]{1,0:T(8,128)S(1)} %get-tuple-element.49), channel_id=1, source_target_pairs={{0,2},{2,0},{1,3},{3,1},{4,6},{6,4},{5,7},{7,5},{8,10},{10,8},{9,1... | collective-permute-start | bytes 208904 | tf_op jit(solution)/shard_map/ppermute | solution.py:576
  81.6 0.6 copy-start.5
  84.7 38.3 %all-to-all-start.1 = ((bf16[64,136,128]{2,1,0:T(8,128)(2,1)}), bf16[64,136,128]{2,1,0:T(8,128)(2,1)}, u32[]{:S(2)}, u32[]{:S(2)}) async-start(bf16[64,136,128]{2,1,0:T(8,128)(2,1)} %split_high.1), calls=%async_computation.1 | async-start | bytes 4456448 | tf_op jit(solution)/shard_map/all_to_all | solution.py:580
  122.9 6.0 %collective-permute-start.4 = (bf16[64,136,128]{2,1,0:T(8,128)(2,1)}, bf16[64,136,128]{2,1,0:T(8,128)(2,1)}, u32[]{:S(2)}, u32[]{:S(2)}) collective-permute-start(bf16[64,136,128]{2,1,0:T(8,128)(2,1)} %all-to-all-done.1.own), channel_id=1, source_target_pairs={{0,1},{1,0},{2,3},{3,2},{4,5},{5,4},{6,7},{7,6},{8,9},{9,8},{10,11... | collective-permute-start | bytes 6684680 | tf_op jit(solution)/shard_map/ppermute | solution.py:624
  122.9 42.3 %all-to-all-start.2 = ((bf16[64,136,128]{2,1,0:T(8,128)(2,1)}), bf16[64,136,128]{2,1,0:T(8,128)(2,1)S(1)}, u32[]{:S(2)}, u32[]{:S(2)}) async-start(bf16[64,136,128]{2,1,0:T(8,128)(2,1)} %split_low.1), calls=%async_computation.2 | async-start | bytes 4456448 | tf_op jit(solution)/shard_map/all_to_all | solution.py:580
  159.9 0.8 copy-start.1
  165.3 4.3 %collective-permute-start.5 = (bf16[64,136,128]{2,1,0:T(8,128)(2,1)S(1)}, bf16[64,136,128]{2,1,0:T(8,128)(2,1)S(1)}, u32[]{:S(2)}, u32[]{:S(2)}) collective-permute-start(bf16[64,136,128]{2,1,0:T(8,128)(2,1)S(1)} %all-to-all-done.2.own), channel_id=1, source_target_pairs={{0,1},{1,0},{2,3},{3,2},{4,5},{5,4},{6,7},{7,6},{8,9},{9,8},{10,11... | collective-permute-start | bytes 6684680 | tf_op jit(solution)/shard_map/ppermute | solution.py:628
  169.6 1.0 copy-start.2
  252.6 16.5 %copy-start.4 = (bf16[1024,2048]{1,0:T(8,128)(2,1)S(1)}, bf16[1024,2048]{1,0:T(8,128)(2,1)}, u32[]{:S(2)}) copy-start(bf16[1024,2048]{1,0:T(8,128)(2,1)} %all-gather.2.cloned.1.call-done) | copy-start | bytes 12582916
  252.6 17.9 %collective-permute-start.7 = (bf16[1024,2048]{1,0:T(8,128)(2,1)}, bf16[1024,2048]{1,0:T(8,128)(2,1)S(1)}, u32[]{:S(2)}, u32[]{:S(2)}) collective-permute-start(bf16[1024,2048]{1,0:T(8,128)(2,1)} %all-gather.2.cloned.1.call-done), channel_id=1, source_target_pairs={{0,1},{1,0},{2,3},{3,2},{4,5},{5,4},{6,7},{7,6},{8,9},{9,8},{10,11... | collective-permute-start | bytes 12582920 | tf_op jit(solution)/shard_map/ppermute | solution.py:632
  259.1 10.0 %collective-permute-start.6 = (bf16[64,2048]{1,0:T(8,128)(2,1)S(1)}, bf16[64,2048]{1,0:T(8,128)(2,1)S(1)}, u32[]{:S(2)}, u32[]{:S(2)}) collective-permute-start(bf16[64,2048]{1,0:T(8,128)(2,1)S(1)} %solve_finish.1), channel_id=1, source_target_pairs={{0,2},{2,0},{1,3},{3,1},{4,6},{6,4},{5,7},{7,5},{8,10},{10,8},{9,1... | collective-permute-start | bytes 786440 | tf_op jit(solution)/shard_map/ppermute | solution.py:631
  271.9 9.3 %collective-permute-start.8 = (bf16[64,2048]{1,0:T(8,128)(2,1)S(1)}, bf16[64,2048]{1,0:T(8,128)(2,1)S(1)}, u32[]{:S(2)}, u32[]{:S(2)}) collective-permute-start(bf16[64,2048]{1,0:T(8,128)(2,1)S(1)} %pad_maximum_fusion), channel_id=1, source_target_pairs={{0,2},{2,0},{1,3},{3,1},{4,6},{6,4},{5,7},{7,5},{8,10},{10,8},{9,1... | collective-permute-start | bytes 786440 | tf_op jit(solution)/shard_map/ppermute | solution.py:642
Sparse Core Ops, SparseCore 0:
  72.5 89.8 all-gather.1
